TPU v7x, 256 devices: a whole 4x4x8 slice. The times are simulated.
256 devices in a mesh: tok: 16 (over y, x), gr: 2 (over z_hi), gc: 8 (over z_lo, core).
Axes of the slice: x: 4, y: 4, z: 8 (z_hi: 2, z_lo: 4; z = z_hi * 4 + z_lo), core: 2. Of those that a mesh axis runs over, the one named last changes fastest.
Arguments:
- acts: bfloat16 [2048, 16384], P('tok', ('gr', 'gc')), may hold values from -24 to 24
- init_basis: float32 [16, 1024, 512], P(('gr', 'gc'), 'tok'), may hold values from -6 to 6
- kept: int32 [16, 16], replicated, may hold values from 0 to 1, as said below
- member: int32 [16], replicated, may hold values from 0 to 1, as said below
Outputs:
- bases: float32 [16, 1024, 512], P(('gr', 'gc'), 'tok')
- latent: bfloat16 [2048, 1024], P(('tok', 'gr', 'gc'))
Inputs may be any that keep to these rules, and one draw needn't show every extreme that they name: kept is symmetric with ones on the diagonal. `member`: each of the 2 group numbers names exactly 8 blocks.
All inputs are finite; a program needn't handle non-finite values.
Results may differ from a plain program's by a relative error of at most 0.0095.
Values may be sent and summed in bfloat16 or wider, within the bound.
A program may use at most 64 MiB of HBM per device.

v0:
```python
import math

import jax
import jax.numpy as jnp
from jax import lax
from jax.sharding import PartitionSpec as P

GBLK = 8
ITERS = 2


ridge = 2.0


def own_solve(lower_own, image):
    solved = [jax.scipy.linalg.solve_triangular(lower_own[0], image[0].T, lower=True).T]
    return jnp.stack(solved)


def per_device(acts, init_basis, kept, member):
    highest = lax.Precision.HIGHEST
    owned = init_basis.shape[0]
    slice_rows = init_basis.shape[1]
    rank_cols = init_basis.shape[2]
    tok_count = lax.axis_size("tok")
    block_cols = slice_rows * tok_count
    tok_rows = acts.shape[0]
    total_tokens = tok_rows * tok_count
    groups = kept.shape[0] // GBLK
    group_cols = GBLK * block_cols
    first = lax.axis_index(("gr", "gc")) * owned
    tok_pos = lax.axis_index("tok")
    links = (member[:, None] == member[None, :]).astype(jnp.int32) * kept
    own_links = lax.dynamic_slice_in_dim(links, first, owned, 0).astype(jnp.bfloat16)
    own_groups = lax.dynamic_slice_in_dim(member, first, owned, 0)
    selector = (own_groups[:, None] == jnp.arange(groups, dtype=jnp.int32)[None, :]).astype(
        jnp.float32
    )
    blocks_x = acts.reshape(tok_rows, owned, block_cols)

    def full_rows(basis_slice):
        return lax.all_gather(basis_slice.astype(jnp.bfloat16), "tok", axis=1, tiled=True)

    basis = init_basis
    basis_bf = full_rows(init_basis)
    for step in range(ITERS):
        proj = jnp.einsum(
            "tob,obr->otr", blocks_x, basis_bf, preferred_element_type=jnp.float32
        ).astype(jnp.bfloat16)
        mixed = jnp.einsum(
            "ok,ktr->otr",
            own_links,
            lax.all_gather(proj, ("gr", "gc"), axis=0, tiled=True),
            preferred_element_type=jnp.float32,
        )
        local_cover = jnp.einsum(
            "tob,otr->obr", blocks_x, mixed.astype(jnp.bfloat16), preferred_element_type=jnp.float32
        )
        summed = lax.psum_scatter(local_cover, "tok", scatter_dimension=1, tiled=True)
        own_rows = lax.dynamic_slice_in_dim(basis_bf, tok_pos * slice_rows, slice_rows, 1)
        image = summed / total_tokens + ridge * own_rows.astype(jnp.float32)
        grams = jnp.einsum("obr,obs->ors", image, image, precision=highest)
        stacked = jnp.einsum("og,ors->grs", selector, grams, precision=highest)
        gram = lax.psum(stacked, ("tok", "gr", "gc"))
        lower = jnp.linalg.cholesky(gram / group_cols)
        own_lower = jnp.einsum("og,grs->ors", selector, lower, precision=highest)
        basis = own_solve(own_lower, image)
        basis_bf = full_rows(basis)
    codes = jnp.einsum("tob,obr->otr", blocks_x, basis_bf, preferred_element_type=jnp.float32)
    placed = jnp.einsum("og,otr->tgr", selector, codes, precision=highest)
    latent = lax.psum_scatter(
        placed.reshape(
            tok_rows // lax.axis_size(("gr", "gc")) * lax.axis_size(("gr", "gc")),
            groups * rank_cols,
        ),
        ("gr", "gc"),
        scatter_dimension=0,
        tiled=True,
    )
    latent = latent * (1.0 / math.sqrt(group_cols))
    return (basis, latent.astype(jnp.bfloat16))


def solution(mesh):
    placed = (P("tok", ("gr", "gc")), P(("gr", "gc"), "tok", None), P(), P())
    return jax.shard_map(
        per_device,
        mesh=mesh,
        in_specs=placed,
        out_specs=(P(("gr", "gc"), "tok", None), P(("tok", "gr", "gc"), None)),
        check_vma=False,
    )
```

profile of v0, /device:TPU:1, one launch (start us, length us, event | category | flops | bytes accessed | tf_op | source)
XLA Modules:
  0.0 1520.8 jit_solution(7414686740243546227)
XLA Ops:
  7.2 1.6 convert_element_type.56
  8.9 52.3 %all-gather.10.cloned.1.call-done = bf16[1,1024,512]{2,1,0:T(8,128)(2,1)} async-done(((bf16[1,64,512]{2,1,0:T(8,128)(2,1)}), bf16[1,1024,512]{2,1,0:T(8,128)(2,1)}) %all-gather.10.cloned.1.call-update) | async-done | bytes 1048592 | tf_op jit(solution)/shard_map/all_gather | solution.py:42
  61.1 2.2 convolution_convert_fusion.1
  65.9 38.5 %all-gather.12.cloned.1.call-done = bf16[2048,512]{1,0:T(8,128)(2,1)} async-done(((bf16[128,512]{1,0:T(8,128)(2,1)}), bf16[2048,512]{1,0:T(8,128)(2,1)}) %all-gather.12.cloned.1.call-update) | async-done | bytes 2097168 | tf_op jit(solution)/shard_map/all_gather | solution.py:53
  104.5 2.9 fusion.2
  107.8 3.7 copy.49
  114.0 94.9 %all-reduce.12.cloned.1.call-done = f32[1,1024,512]{2,0,1:T(1,128)} async-done(((f32[1,1024,512]{2,0,1:T(1,128)}), f32[1,1024,512]{2,0,1:T(1,128)}) %all-reduce.12.cloned.1.call-update) | async-done | bytes 2097168
  209.8 1.9 fusion.38
  211.8 1.7 broadcast_multiply_fusion.3
  214.5 260.7 %all-reduce.8.cloned.1.call-done = f32[2,512,512]{1,2,0:T(8,128)} async-done(((f32[2,512,512]{1,2,0:T(8,128)}), f32[2,512,512]{1,2,0:T(8,128)}) %all-reduce.8.cloned.1.call-update) | async-done | bytes 2097168 | tf_op jit(solution)/shard_map/psum | solution.py:64
  475.2 3.1 broadcast_multiply_fusion.2
  478.3 3.5 copy.52
  481.9 2.1 fusion.1
  485.3 23.5 %custom-call.35 = f32[2,128,128]{2,1,0:T(8,128)S(1)} custom-call(f32[2,128,128]{2,1,0:T(8,128)S(1)} %cholesky.430), custom_call_target="Cholesky" | custom-call | tf_op jit(solution)/shard_map/jit(cholesky)/cholesky | solution.py:65
  508.8 19.7 %custom-call.36 = f32[2,1,128,128]{2,3,1,0:T(8,128)S(1)} custom-call(f32[2,1,128,128]{3,2,1,0:T(8,128)S(1)} %select_bitcast_fusion.5), custom_call_target="InvertDiagBlocksLowerTriangular" | custom-call | tf_op jit(solution)/shard_map/jit(cholesky)/cholesky | solution.py:65
  532.4 24.3 %custom-call.37 = f32[2,128,128]{2,1,0:T(8,128)S(1)} custom-call(f32[2,128,128]{2,1,0:T(8,128)} %cholesky.434), custom_call_target="Cholesky" | custom-call | tf_op jit(solution)/shard_map/jit(cholesky)/cholesky | solution.py:65
  557.4 21.2 %custom-call.38 = f32[2,1,128,128]{2,3,1,0:T(8,128)} custom-call(f32[2,1,128,128]{3,2,1,0:T(8,128)} %get-tuple-element.56), custom_call_target="InvertDiagBlocksLowerTriangular" | custom-call | tf_op jit(solution)/shard_map/jit(cholesky)/cholesky | solution.py:65
  582.1 24.3 %custom-call.39 = f32[2,128,128]{2,1,0:T(8,128)S(1)} custom-call(f32[2,128,128]{2,1,0:T(8,128)} %cholesky.439), custom_call_target="Cholesky" | custom-call | tf_op jit(solution)/shard_map/jit(cholesky)/cholesky | solution.py:65
  607.1 21.1 %custom-call.40 = f32[2,1,128,128]{2,3,1,0:T(8,128)} custom-call(f32[2,1,128,128]{3,2,1,0:T(8,128)} %get-tuple-element.54), custom_call_target="InvertDiagBlocksLowerTriangular" | custom-call | tf_op jit(solution)/shard_map/jit(cholesky)/cholesky | solution.py:65
  630.9 23.7 %custom-call.41 = f32[2,128,128]{2,1,0:T(8,128)S(1)} custom-call(f32[2,128,128]{2,1,0:T(8,128)S(1)} %convolution_subtract_fusion.5), custom_call_target="Cholesky" | custom-call | tf_op jit(solution)/shard_map/jit(cholesky)/cholesky | solution.py:65
  655.3 5.3 fusion.6
  660.8 8.5 while.4
  669.2 39.3 %custom-call.42 = f32[4,128,128]{1,2,0:T(8,128)S(1)} custom-call(f32[4,128,128]{2,1,0:T(8,128)S(1)} %get-tuple-element.18), custom_call_target="InvertDiagBlocksLowerTriangular" | custom-call | tf_op jit(solution)/shard_map/jit(_solve_triangular)/triangular_solve | solution.py:16
  711.0 46.6 %all-gather.14.cloned.1.call-done = bf16[1024,512]{1,0:T(8,128)(2,1)} async-done(((bf16[64,512]{1,0:T(8,128)(2,1)}), bf16[1024,512]{1,0:T(8,128)(2,1)}) %all-gather.14.cloned.1.call-update) | async-done | bytes 1048592 | tf_op jit(solution)/shard_map/all_gather | solution.py:42
  757.6 2.4 fusion.8
  760.0 42.2 %all-gather.16.cloned.1.call-done = bf16[2048,512]{0,1:T(8,128)(2,1)} async-done(((bf16[128,512]{0,1:T(8,128)(2,1)}), bf16[2048,512]{0,1:T(8,128)(2,1)}) %all-gather.16.cloned.1.call-update) | async-done | bytes 2097168 | tf_op jit(solution)/shard_map/all_gather | solution.py:53
  802.2 2.2 copy.85
  805.4 3.7 copy.59
  809.2 98.1 %all-reduce.14.cloned.1.call-done = f32[1,1024,512]{2,0,1:T(1,128)} async-done(((f32[1,1024,512]{2,0,1:T(1,128)}), f32[1,1024,512]{2,0,1:T(1,128)}) %all-reduce.14.cloned.1.call-update) | async-done | bytes 2097168
  908.3 1.9 fusion.33
  910.2 1.7 broadcast_multiply_fusion
  913.2 259.7 %all-reduce.10.cloned.1.call-done = f32[2,512,512]{1,2,0:T(8,128)} async-done(((f32[2,512,512]{1,2,0:T(8,128)}), f32[2,512,512]{1,2,0:T(8,128)}) %all-reduce.10.cloned.1.call-update) | async-done | bytes 2097168 | tf_op jit(solution)/shard_map/psum | solution.py:64
  1172.9 3.1 broadcast_multiply_fusion.1
  1176.1 3.0 copy.62
  1179.1 2.1 fusion
  1182.6 23.5 %custom-call.43 = f32[2,128,128]{2,1,0:T(8,128)S(1)} custom-call(f32[2,128,128]{2,1,0:T(8,128)S(1)} %cholesky.443), custom_call_target="Cholesky" | custom-call | tf_op jit(solution)/shard_map/jit(cholesky)/cholesky | solution.py:65
  1206.1 19.7 %custom-call.44 = f32[2,1,128,128]{2,3,1,0:T(8,128)S(1)} custom-call(f32[2,1,128,128]{3,2,1,0:T(8,128)S(1)} %select_bitcast_fusion.2), custom_call_target="InvertDiagBlocksLowerTriangular" | custom-call | tf_op jit(solution)/shard_map/jit(cholesky)/cholesky | solution.py:65
  1229.7 24.3 %custom-call.45 = f32[2,128,128]{2,1,0:T(8,128)S(1)} custom-call(f32[2,128,128]{2,1,0:T(8,128)} %cholesky.447), custom_call_target="Cholesky" | custom-call | tf_op jit(solution)/shard_map/jit(cholesky)/cholesky | solution.py:65
  1254.7 21.2 %custom-call.46 = f32[2,1,128,128]{2,3,1,0:T(8,128)} custom-call(f32[2,1,128,128]{3,2,1,0:T(8,128)} %get-tuple-element.51), custom_call_target="InvertDiagBlocksLowerTriangular" | custom-call | tf_op jit(solution)/shard_map/jit(cholesky)/cholesky | solution.py:65
  1279.4 24.3 %custom-call.47 = f32[2,128,128]{2,1,0:T(8,128)S(1)} custom-call(f32[2,128,128]{2,1,0:T(8,128)} %cholesky.452), custom_call_target="Cholesky" | custom-call | tf_op jit(solution)/shard_map/jit(cholesky)/cholesky | solution.py:65
  1304.4 21.1 %custom-call.48 = f32[2,1,128,128]{2,3,1,0:T(8,128)} custom-call(f32[2,1,128,128]{3,2,1,0:T(8,128)} %get-tuple-element.49), custom_call_target="InvertDiagBlocksLowerTriangular" | custom-call | tf_op jit(solution)/shard_map/jit(cholesky)/cholesky | solution.py:65
  1328.2 23.7 %custom-call.49 = f32[2,128,128]{2,1,0:T(8,128)S(1)} custom-call(f32[2,128,128]{2,1,0:T(8,128)S(1)} %convolution_subtract_fusion.4), custom_call_target="Cholesky" | custom-call | tf_op jit(solution)/shard_map/jit(cholesky)/cholesky | solution.py:65
  1352.8 5.3 fusion.4
  1358.2 8.5 while.5
  1366.7 39.3 %custom-call.50 = f32[4,128,128]{1,2,0:T(8,128)S(1)} custom-call(f32[4,128,128]{2,1,0:T(8,128)S(1)} %get-tuple-element.19), custom_call_target="InvertDiagBlocksLowerTriangular" | custom-call | tf_op jit(solution)/shard_map/jit(_solve_triangular)/triangular_solve | solution.py:16
  1408.4 46.6 %all-gather.18.cloned.1.call-done = bf16[1024,512]{1,0:T(8,128)(2,1)} async-done(((bf16[64,512]{1,0:T(8,128)(2,1)}), bf16[1024,512]{1,0:T(8,128)(2,1)}) %all-gather.18.cloned.1.call-update) | async-done | bytes 1048592 | tf_op jit(solution)/shard_map/all_gather | solution.py:42
  1455.0 1.7 convolution_bitcast_fusion.2
  1458.7 53.7 %reduce-scatter.2.cloned.1.call-done = f32[8,1024]{1,0:T(8,128)} async-done(((f32[128,1024]{1,0:T(8,128)}), f32[8,1024]{1,0:T(8,128)}) %reduce-scatter.2.cloned.1.call-update) | async-done | bytes 32784 | tf_op jit(solution)/shard_map/reduce_scatter | solution.py:71
  (136 shorter events, 62.7 us)
Async XLA Ops:
  7.2 54.0 %copy-start = (bf16[128,1024]{1,0:T(8,128)(2,1)S(1)}, bf16[128,1024]{1,0:T(8,128)(2,1)}, u32[]{:S(2)}) copy-start(bf16[128,1024]{1,0:T(8,128)(2,1)} %param.7) | copy-start | bytes 786436
  7.2 54.0 %all-gather.10.cloned.1.call-start = ((), (), s32[]{:S(2)}) async-start(), calls=%async_computation.1 | async-start | bytes 1114112 | tf_op jit(solution)/shard_map/all_gather | solution.py:42
  8.8 95.6 %all-gather.12.cloned.1.call-start = ((), (), s32[]{:S(2)}) async-start(), calls=%async_computation.5 | async-start | bytes 2228224 | tf_op jit(solution)/shard_map/all_gather | solution.py:53
  63.4 145.5 %all-reduce.12.cloned.1.call-start = ((), (), s32[]{:S(2)}) async-start(), calls=%async_computation.9 | async-start | bytes 4194304
  111.5 0.7 copy-start.5
  111.6 363.6 %all-reduce.8.cloned.1.call-start = ((), (), s32[]{:S(2)}) async-start(), calls=%async_computation.2 | async-start | bytes 4194304 | tf_op jit(solution)/shard_map/psum | solution.py:64
  213.5 544.1 %all-gather.14.cloned.1.call-start = ((), (), s32[]{:S(2)}) async-start(), calls=%async_computation.6 | async-start | bytes 1114112 | tf_op jit(solution)/shard_map/all_gather | solution.py:42
  478.3 3.5 copy-start.1
  484.0 1.4 copy-start.4
  710.9 91.3 %all-gather.16.cloned.1.call-start = ((), (), s32[]{:S(2)}) async-start(), calls=%async_computation.7 | async-start | bytes 2228224 | tf_op jit(solution)/shard_map/all_gather | solution.py:53
  760.0 147.4 %all-reduce.14.cloned.1.call-start = ((), (), s32[]{:S(2)}) async-start(), calls=%async_computation.10 | async-start | bytes 4194304
  809.2 363.7 %all-reduce.10.cloned.1.call-start = ((), (), s32[]{:S(2)}) async-start(), calls=%async_computation.3 | async-start | bytes 4194304 | tf_op jit(solution)/shard_map/psum | solution.py:64
  911.9 543.1 %all-gather.18.cloned.1.call-start = ((), (), s32[]{:S(2)}) async-start(), calls=%async_computation.8 | async-start | bytes 1114112 | tf_op jit(solution)/shard_map/all_gather | solution.py:42
  1176.1 3.0 copy-start.2
  1181.2 1.4 copy-start.3
  1408.4 104.1 %reduce-scatter.2.cloned.1.call-start = ((), (), s32[]{:S(2)}) async-start(), calls=%async_computation.4 | async-start | bytes 557056 | tf_op jit(solution)/shard_map/reduce_scatter | solution.py:71
Sparse Core Ops, SparseCore 0:
  11.0 50.0 all-gather.9
  63.5 40.8 all-gather.11
  111.7 97.1 all-reduce.11
  215.0 260.1 all-reduce.7
  711.0 46.5 all-gather.13
  760.1 42.0 all-gather.15
  809.3 97.9 all-reduce.13
  912.7 260.1 all-reduce.9
  1408.5 46.5 all-gather.17
  1458.1 54.2 reduce-scatter.1
where the time goes:
time: 1530 us; the launch traced here: 1520 us
  waiting for transfers between devices  993 us (65%)
  other arithmetic  421 us (28%)
  matrix products  45.2 us (3%)
  local copies, waits for them, and re-layouts  44.4 us (3%)
  between operations  15.6 us (1%)
    psum x2, waiting for transfers between devices, per_device(): gram = lax.psum(stacked, ('tok', 'gr', 'gc'))  520 us
    another operation x32, other arithmetic, per_device(): lower = jnp.linalg.cholesky(gram / group_cols)  319 us
    unnamed x12, waiting for transfers between devices  193 us
    all_gather x3, waiting for transfers between devices, full_rows(): lax.all_gather(basis_slice.astype(jnp.bfloat16), 'tok', axis=1, tiled=True)  146 us
    all_gather x2, waiting for transfers between devices, per_device(): lax.all_gather(proj, ('gr', 'gc'), axis=0, tiled=True)  80.7 us
    another operation x6, other arithmetic, own_solve(): jax.scipy.linalg.solve_triangular(lower_own[0], image[0].T, lower=True)  79 us
    reduce_scatter x1, waiting for transfers between devices, per_device(): lax.psum_scatter(placed.reshape(tok_rows // lax.axis_size(('gr', 'gc')) *...  53.7 us
  transfers between devices with their start and end apart: 10, of which 10 were waited for; matrix products, arithmetic and copies ran while one was open for 0% of the time, Pallas kernels for 0%

commit v1 on v0

v1 whole, which is shorter than its diff:
```python
import functools
import math

import jax
import jax.numpy as jnp
from jax import lax
from jax.experimental import pallas as pl
from jax.experimental.pallas import tpu as pltpu
from jax.sharding import PartitionSpec as P

GBLK = 8
ITERS = 2
RIDGE = 2.0
LEAF = 128
MESH = pl.DeviceIdType.MESH
HIGHEST = lax.Precision.HIGHEST
VMEM_LIMIT = 48 * 2**20
F32 = jnp.float32
BF16 = jnp.bfloat16


def vmem():
    return pl.BlockSpec(memory_space=pltpu.VMEM)


def smem():
    return pl.BlockSpec(memory_space=pltpu.SMEM)


def params(collective_id=None):
    if collective_id is None:
        return pltpu.CompilerParams(vmem_limit_bytes=VMEM_LIMIT)
    return pltpu.CompilerParams(
        vmem_limit_bytes=VMEM_LIMIT, collective_id=collective_id, has_side_effects=True
    )


class Place:
    def __init__(self):
        self.tok = lax.axis_size("tok")
        self.gc = lax.axis_size("gc")
        self.line = lax.axis_size("gr") * self.gc
        self.side = math.isqrt(self.tok)
        self.p = lax.axis_index("tok")
        self.gr_at = lax.axis_index("gr")
        self.gc_at = lax.axis_index("gc")
        self.k = self.gr_at * self.gc + self.gc_at
        self.y = self.p // self.side
        self.x = self.p % self.side

    def in_plane(self, p):
        return (p, self.gr_at, self.gc_at)

    def in_line(self, k):
        return (self.p, k // self.gc, k % self.gc)

    def at_axis(self, axis, at):
        if axis == "x":
            return self.in_plane(self.y * self.side + at)
        return self.in_plane(at * self.side + self.x)


def greet(devices):
    barrier = pltpu.get_barrier_semaphore()
    for device in devices:
        pl.semaphore_signal(barrier, inc=1, device_id=device, device_id_type=MESH)
    if devices:
        pl.semaphore_wait(barrier, len(devices))


def line_devices(here):
    return [here.in_line((here.k + d) % here.line) for d in range(1, here.line)]


def plane_devices(here):
    return [here.in_plane((here.p + d) % here.tok) for d in range(1, here.tok)]


def ring_devices(here):
    if here.tok == 1:
        return []
    side = here.side
    return [
        here.at_axis(axis, (at + d) % side)
        for axis, at in (("x", here.x), ("y", here.y))
        for d in (1, side - 1)
    ]


def rcopy(src, dst, send, recv, device):
    return pltpu.make_async_remote_copy(
        src_ref=src, dst_ref=dst, send_sem=send, recv_sem=recv, device_id=device, device_id_type=MESH
    )


class Ring:
    def __init__(self, here, axis, piece, send, recv):
        at = here.x if axis == "x" else here.y
        side = here.side
        self.me, self.right, self.left = at, (at + 1) % side, (at + side - 1) % side
        self.opp = (at + 2) % side
        self.to_right = here.at_axis(axis, self.right)
        self.to_left = here.at_axis(axis, self.left)
        self.piece, self.send, self.recv = piece, send, recv

    def copy(self, slot, owner, part, device):
        ref = self.piece(owner, part)
        return rcopy(ref, ref, self.send.at[slot], self.recv.at[slot], device)

    def start(self):
        self.copy(0, self.me, 0, self.to_right).start()
        self.copy(1, self.me, 1, self.to_left).start()
        self.copy(2, self.me, 1, self.to_right).start()
        self.copy(3, self.me, 0, self.to_left).start()

    def forward(self):
        self.copy(0, self.left, 0, self.to_right).wait_recv()
        self.copy(4, self.left, 0, self.to_right).start()
        self.copy(1, self.right, 1, self.to_left).wait_recv()
        self.copy(5, self.right, 1, self.to_left).start()

    def finish(self):
        self.copy(2, self.left, 1, self.to_right).wait_recv()
        self.copy(3, self.right, 0, self.to_left).wait_recv()
        self.copy(4, self.opp, 0, self.to_right).wait_recv()
        self.copy(5, self.opp, 1, self.to_left).wait_recv()

    def sent(self):
        self.copy(0, self.me, 0, self.to_right).wait_send()
        self.copy(1, self.me, 1, self.to_left).wait_send()
        self.copy(2, self.me, 1, self.to_right).wait_send()
        self.copy(3, self.me, 0, self.to_left).wait_send()
        self.copy(4, self.left, 0, self.to_right).wait_send()
        self.copy(5, self.right, 1, self.to_left).wait_send()


def plane_rings(here, buf, send, recv):
    y, x = here.y, here.x
    return (
        Ring(here, "x", lambda at, part: buf.at[y, at, part], send.at[0], recv.at[0]),
        Ring(here, "y", lambda at, part: buf.at[at, x, 2 + part], send.at[1], recv.at[1]),
        Ring(here, "y", lambda at, part: buf.at[at, :, part], send.at[2], recv.at[2]),
        Ring(here, "x", lambda at, part: buf.at[:, at, 2 + part], send.at[3], recv.at[3]),
    )


def plane_gather_start(here, buf, send, recv):
    if here.tok > 1:
        one_a, one_b, _, _ = plane_rings(here, buf, send, recv)
        one_a.start()
        one_b.start()


def plane_gather_finish(here, buf, send, recv):
    if here.tok > 1:
        one_a, one_b, two_a, two_b = plane_rings(here, buf, send, recv)
        one_a.forward()
        one_b.forward()
        one_a.finish()
        two_a.start()
        one_b.finish()
        two_b.start()
        two_a.forward()
        two_b.forward()
        two_a.finish()
        two_b.finish()


def plane_gather_sent(here, buf, send, recv):
    if here.tok > 1:
        for ring in plane_rings(here, buf, send, recv):
            ring.sent()


def ring_semaphores():
    return [pltpu.SemaphoreType.DMA((4, 6)), pltpu.SemaphoreType.DMA((4, 6))]


def line_semaphores(count):
    return [pltpu.SemaphoreType.DMA((count,)), pltpu.SemaphoreType.DMA((count,))]


def line_copy(here, src, dst, send, recv, to):
    return rcopy(src.at[to], dst.at[here.k], send.at[to], recv.at[here.k], here.in_line(to))


def line_received(here, src, dst, send, recv):
    def body(d, carry):
        other = (here.k + here.line - d) % here.line
        rcopy(
            src.at[other], dst.at[other], send.at[other], recv.at[other], here.in_line(other)
        ).wait_recv()
        return carry

    lax.fori_loop(1, here.line, body, 0)


def line_sent(here, src, dst, send, recv):
    def body(d, carry):
        line_copy(here, src, dst, send, recv, (here.k + d) % here.line).wait_send()
        return carry

    lax.fori_loop(1, here.line, body, 0)


def start_kernel(acts_ref, init_ref, full_ref, basis_ref, out_tiles, in_tiles, xs, xr, bs, br):
    here = Place()
    rows = init_ref.shape[0]
    rank = init_ref.shape[1] // here.tok
    full_ref[here.y, here.x] = acts_ref[...].reshape(full_ref.shape[2:])
    turned = init_ref[...].T
    if here.tok == 1:
        basis_ref[...] = turned.astype(BF16)
        return
    wide = jnp.concatenate([turned, jnp.zeros((turned.shape[0], 128 - rows), F32)], axis=1)
    out_tiles[...] = wide.astype(BF16).reshape(out_tiles.shape)
    greet(plane_devices(here))
    plane_gather_start(here, full_ref, xs, xr)

    def copy(to):
        return rcopy(
            out_tiles.at[to], in_tiles.at[here.p], bs.at[to], br.at[here.p], here.in_plane(to)
        )

    def send(d, carry):
        copy((here.p + d) % here.tok).start()
        return carry

    lax.fori_loop(1, here.tok, send, 0)
    in_tiles[here.p] = out_tiles[here.p]
    plane_gather_finish(here, full_ref, xs, xr)

    def received(d, carry):
        other = (here.p + here.tok - d) % here.tok
        rcopy(
            out_tiles.at[other], in_tiles.at[other], bs.at[other], br.at[other], here.in_plane(other)
        ).wait_recv()
        copy((here.p + d) % here.tok).wait_send()
        return carry

    lax.fori_loop(1, here.tok, received, 0)
    per = 128 // rows
    for c in range(here.tok // per):
        total = in_tiles[c * per].astype(F32)
        for d in range(1, per):
            total += pltpu.roll(in_tiles[c * per + d].astype(F32), d * rows, 1)
        basis_ref[:, c * 128 : c * 128 + 128] = total.astype(BF16)
    plane_gather_sent(here, full_ref, xs, xr)


def start(acts, init):
    tok = lax.axis_size("tok")
    side = math.isqrt(tok)
    tokens, cols = acts.shape
    rows, rank = init.shape
    return pl.pallas_call(
        start_kernel,
        out_shape=(
            jax.ShapeDtypeStruct((side, side, 4, tokens // 4, cols), BF16),
            jax.ShapeDtypeStruct((rank // tok, cols), BF16),
        ),
        in_specs=[vmem(), vmem()],
        out_specs=(vmem(), vmem()),
        scratch_shapes=[
            pltpu.VMEM((tok, rank // tok, 128), BF16),
            pltpu.VMEM((tok, rank // tok, 128), BF16),
            *ring_semaphores(),
            *line_semaphores(tok),
        ],
        compiler_params=params(0),
    )(acts, init)


def step_kernel(
    links_ref, same_ref, acts_ref, basis_ref,
    image_ref, gram_ref,
    proj_out, proj_in, mixed_out, mixed_in, wide, part_out, part_in, sum_out, sum_in,
    ps, pr, ms, mr, is_, ir, gs, gr, ss, sr, hs, hr,
):
    here = Place()
    line = here.line
    tokens, cols = acts_ref.shape
    rank = basis_ref.shape[0]
    chunk = tokens // line
    greet(line_devices(here) + ring_devices(here))

    per = 2 if line % 2 == 0 else 1
    groups = line // per

    def project(d, carry):
        u = (here.k // per + 1 + d) % groups
        at = pl.multiple_of(u * (per * chunk), per * chunk)
        proj = lax.dot_general(
            basis_ref[...], acts_ref[pl.ds(at, per * chunk), :],
            (((1,), (1,)), ((), ())), preferred_element_type=F32,
        ).astype(BF16)
        for v in range(per):
            c = u * per + v
            proj_out[c] = proj[:, v * chunk : (v + 1) * chunk]

            @pl.when(c != here.k)
            def _():
                line_copy(here, proj_out, proj_in, ps, pr, c).start()

        return carry

    lax.fori_loop(0, groups, project, 0)
    proj_in[here.k] = proj_out[here.k]
    line_received(here, proj_out, proj_in, ps, pr)
    for j in range(line):
        wide[j] = proj_in[j].astype(F32)

    def mix(d, carry):
        i = (here.k + 1 + d) % line
        total = links_ref[i, 0] * wide[0]
        for j in range(1, line):
            total += links_ref[i, j] * wide[j]
        mixed_out[i] = total.astype(BF16)

        @pl.when(i != here.k)
        def _():
            line_copy(here, mixed_out, mixed_in, ms, mr, i).start()

        return carry

    lax.fori_loop(0, line, mix, 0)
    mixed_in[here.k] = mixed_out[here.k]
    line_received(here, mixed_out, mixed_in, ms, mr)
    mixed = jnp.concatenate([mixed_in[c] for c in range(line)], axis=1)
    image = jnp.dot(mixed, acts_ref[...], preferred_element_type=F32)
    image = image * (1.0 / tokens) + RIDGE * basis_ref[...].astype(F32)
    image_ref[here.y, here.x] = image.reshape(image_ref.shape[2:])
    plane_gather_start(here, image_ref, is_, ir)
    plane_gather_finish(here, image_ref, is_, ir)

    whole = image_ref[...].reshape(rank * here.tok, cols)
    gram = lax.dot_general(
        image, whole, (((1,), (1,)), ((), ())), precision=HIGHEST, preferred_element_type=F32
    )
    high, across = part_out.shape[1:]
    down = rank // high
    over = gram.shape[1] // across
    for a in range(down):
        for b in range(over):
            part_out[a * over + b] = gram[a * high : (a + 1) * high, b * across : (b + 1) * across]

    def send_part(d, carry):
        line_copy(here, part_out, part_in, gs, gr, (here.k + d) % line).start()
        return carry

    lax.fori_loop(1, line, send_part, 0)
    part_in[here.k] = part_out[here.k]
    line_received(here, part_out, part_in, gs, gr)

    def add(d, carry):
        i = (here.k + 1 + d) % line
        total = same_ref[i, 0] * part_in[0]
        for j in range(1, line):
            total += same_ref[i, j] * part_in[j]
        sum_out[i] = total

        @pl.when(i != here.k)
        def _():
            line_copy(here, sum_out, sum_in, ss, sr, i).start()

        return carry

    lax.fori_loop(0, line, add, 0)
    sum_in[here.k] = sum_out[here.k]
    line_received(here, sum_out, sum_in, ss, sr)
    rows = [
        jnp.concatenate([sum_in[a * over + b] for b in range(over)], axis=1) for a in range(down)
    ]
    gram_ref[here.y, here.x] = jnp.concatenate(rows, axis=0).reshape(gram_ref.shape[2:])
    plane_gather_start(here, gram_ref, hs, hr)
    plane_gather_finish(here, gram_ref, hs, hr)

    line_sent(here, proj_out, proj_in, ps, pr)
    line_sent(here, mixed_out, mixed_in, ms, mr)
    line_sent(here, part_out, part_in, gs, gr)
    line_sent(here, sum_out, sum_in, ss, sr)
    plane_gather_sent(here, image_ref, is_, ir)
    plane_gather_sent(here, gram_ref, hs, hr)


def step(links, same, acts, basis):
    tok = lax.axis_size("tok")
    line = lax.axis_size("gr") * lax.axis_size("gc")
    side = math.isqrt(tok)
    tokens, cols = acts.shape
    rank = basis.shape[0]
    chunk = tokens // line
    high = max(8, rank // line)
    across = rank * rank * tok // line // high
    pieces = (line, rank, chunk)
    tiles = (line, high, across)
    image, gram = pl.pallas_call(
        step_kernel,
        out_shape=(
            jax.ShapeDtypeStruct((side, side, 4, rank // 4, cols), F32),
            jax.ShapeDtypeStruct((side, side, 4, rank // 4, rank * tok), F32),
        ),
        in_specs=[smem(), smem(), vmem(), vmem()],
        out_specs=(vmem(), vmem()),
        scratch_shapes=[
            pltpu.VMEM(pieces, BF16),
            pltpu.VMEM(pieces, BF16),
            pltpu.VMEM(pieces, BF16),
            pltpu.VMEM(pieces, BF16),
            pltpu.VMEM(pieces, F32),
            pltpu.VMEM(tiles, F32),
            pltpu.VMEM(tiles, F32),
            pltpu.VMEM(tiles, F32),
            pltpu.VMEM(tiles, F32),
            *line_semaphores(line),
            *line_semaphores(line),
            *ring_semaphores(),
            *line_semaphores(line),
            *line_semaphores(line),
            *ring_semaphores(),
        ],
        compiler_params=params(1),
    )(links, same, acts, basis)
    return image.reshape(rank * tok, cols), gram.reshape(rank * tok, rank * tok)


def leaf_inverse(tiles):
    shape = tiles[0].shape
    lane = lax.broadcasted_iota(jnp.int32, shape, 1)
    sub = lax.broadcasted_iota(jnp.int32, shape, 0)
    tiles = list(tiles)
    count = len(tiles)
    for s in range(count):
        c0 = 8 * s
        here = tiles[s]
        cols = [jnp.broadcast_to(here[:, c0 + j : c0 + j + 1], shape) for j in range(8)]
        diag = (lane >= c0) & (lane < c0 + 8)
        first = jnp.where(diag, jnp.where(lane - c0 == sub, 1.0, 0.0), here)
        full, low = first, first
        pivots = jnp.ones(shape, F32)
        for j in range(8):
            pivot = jnp.broadcast_to(cols[j][j : j + 1, :], shape)
            ratio = cols[j] * (1.0 / pivot)
            others = jnp.where(sub == j, 0.0, ratio)
            below = jnp.where(sub > j, ratio, 0.0)
            for k in range(j + 1, 8):
                cols[k] = cols[k] - others * jnp.broadcast_to(cols[k][j : j + 1, :], shape)
            full = full - others * jnp.broadcast_to(full[j : j + 1, :], shape)
            low = low - below * jnp.broadcast_to(low[j : j + 1, :], shape)
            pivots = jnp.where(sub == j, pivot, pivots)
        solved = full / pivots
        tiles[s] = jnp.where(lane < c0 + 8, low * lax.rsqrt(pivots), 0.0)
        rows = [jnp.broadcast_to(solved[k : k + 1, :], shape) for k in range(8)]
        for t in range(s + 1, count):
            old = tiles[t]
            new = jnp.where(diag, 0.0, old)
            for k in range(8):
                new = new - jnp.broadcast_to(old[:, c0 + k : c0 + k + 1], shape) * rows[k]
            tiles[t] = new
    return jnp.concatenate(tiles, axis=0)


def dot(a, b):
    return jnp.dot(a, b, precision=HIGHEST, preferred_element_type=F32)


def factor_inverse(m_ref, w_ref):
    size = m_ref.shape[0]
    for r0 in range(0, size, LEAF):
        r1 = r0 + LEAF
        inv = leaf_inverse([m_ref[r0 + 8 * t : r0 + 8 * t + 8, r0:r1] for t in range(LEAF // 8)])
        w_ref[r0:r1, r0:r1] = inv
        if r0:
            left = dot(inv, m_ref[r0:r1, :r0])
            w_ref[r0:r1, :r0] = left
        if r1 < size:
            w_ref[r0:r1, r1:] = jnp.zeros((LEAF, size - r1), F32)
            right = dot(inv, m_ref[r0:r1, r1:])
            back = right.T
            m_ref[r1:, r1:] = m_ref[r1:, r1:] - dot(back, right)
            m_ref[r1:, r0:r1] = -dot(back, inv)
            if r0:
                m_ref[r1:, :r0] = m_ref[r1:, :r0] - dot(back, left)


def slice_kernel(scale, gram_ref, image_ref, basis_ref, m_ref, w_ref):
    rank = basis_ref.shape[0]
    m_ref[...] = gram_ref[...] * scale
    factor_inverse(m_ref, w_ref)
    at = pl.multiple_of(lax.axis_index("tok") * rank, rank)
    basis_ref[...] = dot(w_ref[pl.ds(at, rank), :], image_ref[...]).astype(BF16)


def next_basis(gram, image, group_cols):
    rank = gram.shape[0]
    return pl.pallas_call(
        functools.partial(slice_kernel, 1.0 / group_cols),
        out_shape=jax.ShapeDtypeStruct((rank // lax.axis_size("tok"), image.shape[1]), BF16),
        in_specs=[vmem(), vmem()],
        out_specs=vmem(),
        scratch_shapes=[pltpu.VMEM((rank, rank), F32), pltpu.VMEM((rank, rank), F32)],
        compiler_params=params(),
    )(gram, image)


def last_kernel(scale, gram_ref, image_ref, acts_ref, bases_ref, codes_ref, m_ref, w_ref, turned):
    rows = bases_ref.shape[0]
    cols = image_ref.shape[1]
    m_ref[...] = gram_ref[...] * scale
    factor_inverse(m_ref, w_ref)
    basis = dot(w_ref[...], image_ref[...])
    codes_ref[...] = lax.dot_general(
        acts_ref[...], basis.astype(BF16), (((1,), (1,)), ((), ())), preferred_element_type=F32
    )
    wide = turned.shape[0]
    per = wide // rows
    p = lax.axis_index("tok")
    at = pl.multiple_of(p // per * wide, wide)
    turned[...] = dot(w_ref[...], image_ref[:, pl.ds(at, wide)]).T
    bases_ref[...] = turned[pl.ds(pl.multiple_of(p % per * rows, rows), rows), :]


def last(gram, image, acts, rows, group_cols):
    rank = gram.shape[0]
    return pl.pallas_call(
        functools.partial(last_kernel, 1.0 / group_cols),
        out_shape=(
            jax.ShapeDtypeStruct((rows, rank), F32),
            jax.ShapeDtypeStruct((acts.shape[0], rank), F32),
        ),
        in_specs=[vmem(), vmem(), vmem()],
        out_specs=(vmem(), vmem()),
        scratch_shapes=[
            pltpu.VMEM((rank, rank), F32),
            pltpu.VMEM((rank, rank), F32),
            pltpu.VMEM((max(rows, 128), rank), F32),
        ],
        compiler_params=params(),
    )(gram, image, acts)


def latent_kernel(scale, groups, select_ref, codes_ref, out_ref, in_tiles, send, recv):
    here = Place()
    rank = codes_ref.shape[2]
    greet(line_devices(here))

    def go(d, carry):
        line_copy(here, codes_ref, in_tiles, send, recv, (here.k + d) % here.line).start()
        return carry

    lax.fori_loop(1, here.line, go, 0)
    in_tiles[here.k] = codes_ref[here.k]
    line_received(here, codes_ref, in_tiles, send, recv)
    for g in range(groups):
        total = select_ref[g, 0] * in_tiles[0]
        for j in range(1, here.line):
            total += select_ref[g, j] * in_tiles[j]
        out_ref[:, g * rank : (g + 1) * rank] = (total * scale).astype(BF16)
    line_sent(here, codes_ref, in_tiles, send, recv)


def latent_of(select, codes, group_cols):
    groups, line = select.shape
    tokens, rank = codes.shape
    tiles = (line, tokens // line, rank)
    return pl.pallas_call(
        functools.partial(latent_kernel, 1.0 / math.sqrt(group_cols), groups),
        out_shape=jax.ShapeDtypeStruct((tokens // line, groups * rank), BF16),
        in_specs=[smem(), vmem()],
        out_specs=vmem(),
        scratch_shapes=[pltpu.VMEM(tiles, F32), *line_semaphores(line)],
        compiler_params=params(2),
    )(select, codes.reshape(tiles))


def per_device(acts, init_basis, kept, member):
    tok = lax.axis_size("tok")
    groups = kept.shape[0] // GBLK
    rows = init_basis.shape[1]
    group_cols = GBLK * rows * tok
    equal = member[:, None] == member[None, :]
    same = equal.astype(F32)
    links = jnp.where(equal, kept, 0).astype(F32)
    select = (member[None, :] == jnp.arange(groups, dtype=jnp.int32)[:, None]).astype(F32)
    full, basis = start(acts, init_basis[0])
    full = full.reshape(acts.shape[0] * tok, acts.shape[1])
    for turn in range(ITERS):
        image, gram = step(links, same, full, basis)
        if turn < ITERS - 1:
            basis = next_basis(gram, image, group_cols)
    bases, codes = last(gram, image, acts, rows, group_cols)
    return bases[None], latent_of(select, codes, group_cols)


def solution(mesh):
    placed = (P("tok", ("gr", "gc")), P(("gr", "gc"), "tok", None), P(), P())
    return jax.shard_map(
        per_device,
        mesh=mesh,
        in_specs=placed,
        out_specs=(P(("gr", "gc"), "tok", None), P(("tok", "gr", "gc"), None)),
        check_vma=False,
    )
```

time: 1530 us -> 256 us (0.17)
  waiting for transfers between devices: 993 us -> 0 us
  other arithmetic: 421 us -> 1.61 us
  Pallas kernels: 0 us -> 246 us
  matrix products: 45.2 us -> 0 us
  local copies, waits for them, and re-layouts: 44.4 us -> 4.4 us
    psum x2 -> x0, waiting for transfers between devices: 520 us -> none  [per_device(): gram = lax.psum(stacked, ('tok', 'gr', 'gc'))]
    another operation x41 -> x0, other arithmetic: 400 us -> none  [the longest x32 319 us: per_device(): lower = jnp.linalg.cholesky(gram / group_cols)]
    pallas_call x0 -> x6, Pallas kernels: none -> 246 us  [the longest x2 136 us: step(): pl.pallas_call(step_kernel, out_shape=(jax.ShapeDtypeStruct((side, side,...]
    all_gather x5 -> x0, waiting for transfers between devices: 226 us -> none  [the longest x3 146 us: full_rows(): lax.all_gather(basis_slice.astype(jnp.bfloat16), 'tok', axis=1, tiled=True)]
    unnamed x12 -> x0, waiting for transfers between devices: 193 us -> none
    reduce_scatter x1 -> x0, waiting for transfers between devices: 53.7 us -> none  [per_device(): lax.psum_scatter(placed.reshape(tok_rows // lax.axis_size(('gr', 'gc')) *...]
    dot_general x11 -> x0, matrix products: 24.9 us -> none  [the longest x2 10.5 us: per_device(): own_lower = jnp.einsum('og,grs->ors', selector, lower, precision=highest)]
    another operation x26 -> x0, matrix products: 20.3 us -> none  [the longest x12 17.1 us: per_device(): lower = jnp.linalg.cholesky(gram / group_cols)]
  transfers between devices with their start and end apart: 10 -> 0, of which waited for: 10 -> 0; matrix products, arithmetic and copies ran while one was open for 0% -> 0% of each run, Pallas kernels for 0% -> 0%
where the time goes in v1:
time: 256 us; the launch traced here: 253 us
  Pallas kernels  246 us (96%)
  local copies, waits for them, and re-layouts  4.4 us (2%)
    pallas_call x2, Pallas kernels, step(): pl.pallas_call(step_kernel, out_shape=(jax.ShapeDtypeStruct((side, side,...  136 us
    pallas_call x1, Pallas kernels, next_basis(): pl.pallas_call(functools.partial(slice_kernel, 1.0 / group_cols), out_sha...  34.3 us
    pallas_call x1, Pallas kernels, start(): pl.pallas_call(start_kernel, out_shape=(jax.ShapeDtypeStruct((side, side,...  30.9 us
    pallas_call x1, Pallas kernels, last(): pl.pallas_call(functools.partial(last_kernel, 1.0 / group_cols), out_shap...  27.8 us
    pallas_call x1, Pallas kernels, latent_of(): pl.pallas_call(functools.partial(latent_kernel, 1.0 / math.sqrt(group_col...  16.7 us

profile of v1, /device:TPU:1, one launch (start us, length us, event | category | flops | bytes accessed | tf_op | source)
XLA Modules:
  0.0 252.9 jit_solution(15930551400912373955)
XLA Ops:
  0.6 0.0 copy-start.1
  0.6 0.9 copy-done.1
  1.6 0.0 copy-start.3
  1.6 0.9 copy-done.3
  2.5 30.9 %shard_map.59 = (bf16[4,4,4,32,1024]{4,3,2,1,0:T(8,128)(2,1)S(1)}, bf16[32,1024]{1,0:T(8,128)(2,1)S(1)}) custom-call(bf16[128,1024]{1,0:T(8,128)(2,1)S(1)} %copy-done.1, f32[64,512]{1,0:T(8,128)S(1)} %bitcast.15), custom_call_target="tpu_custom_call" | custom-call | tf_op jit(solution)/shard_map/pallas_call | solution.py:256
  33.4 0.0 copy-start
  33.4 1.9 copy-done
  35.4 0.8 compare_convert_fusion.same_ref
  36.2 0.8 fusion.links_ref
  37.0 72.2 %shard_map.60 = (f32[4,4,4,8,1024]{4,3,2,1,0:T(8,128)S(1)}, f32[4,4,4,8,512]{4,3,2,1,0:T(8,128)S(1)}) custom-call(f32[16,16]{1,0:T(8,128)S(1)} %fusion.links_ref, f32[16,16]{1,0:T(8,128)S(1)} %compare_convert_fusion.same_ref, bf16[2048,1024]{1,0:T(8,128)(2,1)} %bitcast.8, bf16[32,1024]{1,0:T(8,128)(2,1)S(1)} %get-tuple-element.11.basis_ref), custom_call_target="tpu_custom_call" | custom-call | tf_op jit(solution)/shard_map/pallas_call | solution.py:397
  109.2 34.3 %shard_map.61.basis_ref = bf16[32,1024]{1,0:T(8,128)(2,1)S(1)} custom-call(f32[512,512]{1,0:T(8,128)S(1)} %bitcast.12, f32[512,1024]{1,0:T(8,128)S(1)} %bitcast.10), custom_call_target="tpu_custom_call" | custom-call | tf_op jit(solution)/shard_map/pallas_call | solution.py:496
  143.5 0.0 copy-start.2
  143.5 64.1 %shard_map.62 = (f32[4,4,4,8,1024]{4,3,2,1,0:T(8,128)S(1)}, f32[4,4,4,8,512]{4,3,2,1,0:T(8,128)S(1)}) custom-call(f32[16,16]{1,0:T(8,128)S(1)} %fusion.links_ref, f32[16,16]{1,0:T(8,128)S(1)} %compare_convert_fusion.same_ref, bf16[2048,1024]{1,0:T(8,128)(2,1)} %bitcast.9, bf16[32,1024]{1,0:T(8,128)(2,1)S(1)} %shard_map.61.basis_ref), custom_call_target="tpu_custom_call" | custom-call | tf_op jit(solution)/shard_map/pallas_call | solution.py:397
  207.6 0.0 copy-start.4
  207.6 0.0 copy-done.2
  207.6 27.8 %shard_map.63 = (f32[64,512]{1,0:T(8,128)}, f32[128,512]{1,0:T(8,128)S(1)}) custom-call(f32[512,512]{1,0:T(8,128)S(1)} %bitcast.13, f32[512,1024]{1,0:T(8,128)S(1)} %bitcast.11, bf16[128,1024]{1,0:T(8,128)(2,1)S(1)} %copy-done.2), custom_call_target="tpu_custom_call" | custom-call | tf_op jit(solution)/shard_map/pallas_call | solution.py:525
  235.4 0.0 copy-done.4
  235.4 16.7 %shard_map.64 = bf16[8,1024]{1,0:T(8,128)(2,1)S(1)} custom-call(f32[2,16]{1,0:T(2,128)S(1)} %compare_convert_fusion.1.select_ref, f32[16,8,512]{2,1,0:T(8,128)S(1)} %bitcast.14), custom_call_target="tpu_custom_call" | custom-call | tf_op jit(solution)/shard_map/pallas_call | solution.py:566
  252.1 0.6 copy.7
  (1 shorter events, 0.0 us)
Async XLA Ops:
  0.6 1.0 copy-start.1
  1.6 0.9 copy-start.3
  33.4 1.9 copy-start
  143.5 64.1 %copy-start.2 = (bf16[128,1024]{1,0:T(8,128)(2,1)S(1)}, bf16[128,1024]{1,0:T(8,128)(2,1)}, u32[]{:S(2)}) copy-start(bf16[128,1024]{1,0:T(8,128)(2,1)} %acts_ref.3) | copy-start | bytes 786436
  207.6 27.8 %copy-start.4 = (s32[16]{0:T(128)S(1)}, s32[16]{0:T(128)}, u32[]{:S(2)}) copy-start(s32[16]{0:T(128)} %param.7) | copy-start | bytes 196

commit v2 on v0

v2 whole, which is shorter than its diff:
```python
import functools
import math

import jax
import jax.numpy as jnp
from jax import lax
from jax.experimental import pallas as pl
from jax.experimental.pallas import tpu as pltpu
from jax.sharding import PartitionSpec as P

GBLK = 8
ITERS = 2
RIDGE = 2.0
LEAF = 128
MESH = pl.DeviceIdType.MESH
HIGHEST = lax.Precision.HIGHEST
VMEM_LIMIT = 48 * 2**20
F32 = jnp.float32
BF16 = jnp.bfloat16


def vmem():
    return pl.BlockSpec(memory_space=pltpu.VMEM)


def smem():
    return pl.BlockSpec(memory_space=pltpu.SMEM)


def params(collective_id=None):
    if collective_id is None:
        return pltpu.CompilerParams(vmem_limit_bytes=VMEM_LIMIT)
    return pltpu.CompilerParams(
        vmem_limit_bytes=VMEM_LIMIT, collective_id=collective_id, has_side_effects=True
    )


class Place:
    def __init__(self):
        self.tok = lax.axis_size("tok")
        self.gc = lax.axis_size("gc")
        self.line = lax.axis_size("gr") * self.gc
        self.side = math.isqrt(self.tok)
        self.p = lax.axis_index("tok")
        self.gr_at = lax.axis_index("gr")
        self.gc_at = lax.axis_index("gc")
        self.k = self.gr_at * self.gc + self.gc_at
        self.y = self.p // self.side
        self.x = self.p % self.side

    def in_plane(self, p):
        return (p, self.gr_at, self.gc_at)

    def in_line(self, k):
        return (self.p, k // self.gc, k % self.gc)

    def at_axis(self, axis, at):
        if axis == "x":
            return self.in_plane(self.y * self.side + at)
        return self.in_plane(at * self.side + self.x)


def greet(devices):
    barrier = pltpu.get_barrier_semaphore()
    for device in devices:
        pl.semaphore_signal(barrier, inc=1, device_id=device, device_id_type=MESH)
    if devices:
        pl.semaphore_wait(barrier, len(devices))


def line_devices(here):
    return [here.in_line((here.k + d) % here.line) for d in range(1, here.line)]


def plane_devices(here):
    return [here.in_plane((here.p + d) % here.tok) for d in range(1, here.tok)]


def ring_devices(here):
    if here.tok == 1:
        return []
    side = here.side
    return [
        here.at_axis(axis, (at + d) % side)
        for axis, at in (("x", here.x), ("y", here.y))
        for d in (1, side - 1)
    ]


def rcopy(src, dst, send, recv, device):
    return pltpu.make_async_remote_copy(
        src_ref=src, dst_ref=dst, send_sem=send, recv_sem=recv, device_id=device, device_id_type=MESH
    )


class Ring:
    def __init__(self, here, axis, piece, send, recv):
        at = here.x if axis == "x" else here.y
        side = here.side
        self.me, self.right, self.left = at, (at + 1) % side, (at + side - 1) % side
        self.opp = (at + 2) % side
        self.to_right = here.at_axis(axis, self.right)
        self.to_left = here.at_axis(axis, self.left)
        self.piece, self.send, self.recv = piece, send, recv

    def copy(self, slot, owner, part, device):
        ref = self.piece(owner, part)
        return rcopy(ref, ref, self.send.at[slot], self.recv.at[slot], device)

    def start(self):
        self.copy(0, self.me, 0, self.to_right).start()
        self.copy(1, self.me, 1, self.to_left).start()
        self.copy(2, self.me, 1, self.to_right).start()
        self.copy(3, self.me, 0, self.to_left).start()

    def forward(self):
        self.copy(0, self.left, 0, self.to_right).wait_recv()
        self.copy(4, self.left, 0, self.to_right).start()
        self.copy(1, self.right, 1, self.to_left).wait_recv()
        self.copy(5, self.right, 1, self.to_left).start()

    def finish(self):
        self.copy(2, self.left, 1, self.to_right).wait_recv()
        self.copy(3, self.right, 0, self.to_left).wait_recv()
        self.copy(4, self.opp, 0, self.to_right).wait_recv()
        self.copy(5, self.opp, 1, self.to_left).wait_recv()

    def sent(self):
        self.copy(0, self.me, 0, self.to_right).wait_send()
        self.copy(1, self.me, 1, self.to_left).wait_send()
        self.copy(2, self.me, 1, self.to_right).wait_send()
        self.copy(3, self.me, 0, self.to_left).wait_send()
        self.copy(4, self.left, 0, self.to_right).wait_send()
        self.copy(5, self.right, 1, self.to_left).wait_send()


def plane_rings(here, buf, send, recv):
    y, x = here.y, here.x
    return (
        Ring(here, "x", lambda at, part: buf.at[y, at, part], send.at[0], recv.at[0]),
        Ring(here, "y", lambda at, part: buf.at[at, x, 2 + part], send.at[1], recv.at[1]),
        Ring(here, "y", lambda at, part: buf.at[at, :, part], send.at[2], recv.at[2]),
        Ring(here, "x", lambda at, part: buf.at[:, at, 2 + part], send.at[3], recv.at[3]),
    )


def plane_gather_start(here, buf, send, recv):
    if here.tok > 1:
        one_a, one_b, _, _ = plane_rings(here, buf, send, recv)
        one_a.start()
        one_b.start()


def plane_gather_finish(here, buf, send, recv):
    if here.tok > 1:
        one_a, one_b, two_a, two_b = plane_rings(here, buf, send, recv)
        one_a.forward()
        one_b.forward()
        one_a.finish()
        two_a.start()
        one_b.finish()
        two_b.start()
        two_a.forward()
        two_b.forward()
        two_a.finish()
        two_b.finish()


def plane_gather_sent(here, buf, send, recv):
    if here.tok > 1:
        for ring in plane_rings(here, buf, send, recv):
            ring.sent()


def group_copy(src, dst, sems, which, device):
    return rcopy(src, dst, sems.at[0, which], sems.at[1, which], device)


class Exchange:
    def __init__(self, at, count, device, src, dst, sems, which):
        self.at, self.count, self.device = at, count, device
        self.src, self.dst, self.sems, self.which = src, dst, sems, which

    def send(self, to):
        group_copy(
            self.src.at[to], self.dst.at[self.at], self.sems, self.which, self.device(to)
        ).start()

    def send_all(self):
        def body(d, carry):
            self.send(lax.rem(self.at + d, self.count))
            return carry

        lax.fori_loop(1, self.count, body, 0)

    def keep(self):
        self.dst[self.at] = self.src[self.at]

    def all_of(self, ref, number):
        other = lax.rem(self.at + 1, self.count)
        return group_copy(
            ref.at[pl.ds(0, number)], ref.at[pl.ds(0, number)], self.sems, self.which, self.device(other)
        )

    def received(self, number=None):
        number = self.count - 1 if number is None else number
        if number:
            self.all_of(self.dst, number).wait_recv()

    def sent(self, number=None):
        number = self.count - 1 if number is None else number
        if number:
            self.all_of(self.src, number).wait_send()


def leaf_inverse(block):
    count, high, wide = block.shape
    shape = (high, wide)
    lane = lax.broadcasted_iota(jnp.int32, shape, 1)
    sub = lax.broadcasted_iota(jnp.int32, shape, 0)

    def down(v, r):
        return jnp.broadcast_to(v[r : r + 1, :], shape)

    done = []
    rest = block
    for s in range(count):
        c0 = 8 * s
        here = rest[0]
        cols = [jnp.broadcast_to(here[:, c0 + j : c0 + j + 1], shape) for j in range(8)]
        diag = (lane >= c0) & (lane < c0 + 8)
        first = jnp.where(diag, jnp.where(lane - c0 == sub, 1.0, 0.0), here)
        full, low = first, first
        pivots = jnp.ones(shape, F32)
        for j in range(8):
            pivot = down(cols[j], j)
            inverse = 1.0 / pivot
            others = jnp.where(sub == j, 0.0, cols[j])
            below = jnp.where(sub > j, cols[j], 0.0)
            for k in range(j + 1, 8):
                cols[k] = cols[k] - (others * down(cols[k], j)) * inverse
            full = full - (others * down(full, j)) * inverse
            low = low - (below * down(low, j)) * inverse
            pivots = jnp.where(sub == j, pivot, pivots)
        solved = full / pivots
        done.append(jnp.where(lane < c0 + 8, low * lax.rsqrt(pivots), 0.0))
        if s + 1 < count:
            old = rest[1:]
            terms = [
                jnp.broadcast_to(old[:, :, c0 + k : c0 + k + 1], old.shape) * down(solved, k)[None]
                for k in range(8)
            ]
            while len(terms) > 1:
                terms = [terms[i] + terms[i + 1] for i in range(0, len(terms), 2)]
            rest = jnp.where(diag[None], 0.0, old) - terms[0]
    return jnp.stack(done)


def dot(a, b):
    return jnp.dot(a, b, precision=HIGHEST, preferred_element_type=F32)


def dot_t(a, b):
    return lax.dot_general(
        a, b, (((1,), (1,)), ((), ())), precision=HIGHEST, preferred_element_type=F32
    )


def factor_inverse(m_ref, w_ref):
    size = m_ref.shape[0]
    w_ref[...] = jnp.zeros(w_ref.shape, F32)

    def turn(step, carry):
        at = pl.ds(pl.multiple_of(step * LEAF, LEAF), LEAF)
        w_ref[at, at] = leaf_inverse(m_ref[at, at].reshape(LEAF // 8, 8, LEAF)).reshape(LEAF, LEAF)
        for b in range(size // LEAF):
            r0, r1 = b * LEAF, (b + 1) * LEAF

            @pl.when(step == b)
            def _():
                inv = w_ref[r0:r1, r0:r1]
                if r0:
                    left = dot(inv, m_ref[r0:r1, :r0])
                    w_ref[r0:r1, :r0] = left
                if r1 < size:
                    back = dot_t(m_ref[r1:, r0:r1], inv)
                    for c in range(r1, size, LEAF):
                        m_ref[c:, c : c + LEAF] -= dot_t(
                            back[c - r1 :], back[c - r1 : c - r1 + LEAF]
                        )
                    m_ref[r1:, r0:r1] = -dot(back, inv)
                    if r0:
                        m_ref[r1:, :r0] -= dot(back, left)

        return carry

    lax.fori_loop(0, size // LEAF, turn, 0)


def tokens_at(full_ref, u, size):
    side, _, _, quarter, cols = full_ref.shape
    shard = 4 * quarter
    if size >= shard:
        m = size // shard
        if m <= side:
            part = full_ref[u * m // side, pl.ds(u * m % side, m)]
        else:
            part = full_ref[pl.ds(u * (m // side), m // side)]
    else:
        per = quarter // size
        part = full_ref[0, 0, u // per, pl.ds(u % per * size, size)]
    return part.reshape(size, cols)


def eight_rows(image_ref, row):
    side, _, _, quarter, _ = image_ref.shape
    shard, within = row // (4 * quarter), row % (4 * quarter)
    place = (shard // side, shard % side, within // quarter)
    if quarter == 8:
        return image_ref[place]
    return image_ref[(*place, pl.ds(pl.multiple_of(within % quarter, 8), 8))]


def masks(member_ref, line, groups):
    rows = lax.broadcasted_iota(jnp.int32, (line, line), 0)
    across = lax.broadcasted_iota(jnp.int32, (line, line), 1)
    row = jnp.broadcast_to(member_ref[...].astype(F32), (line, line))
    column = jnp.sum(jnp.where(rows == across, row, 0.0), axis=1, keepdims=True)
    wide = jnp.broadcast_to(column, (line, 128))
    spread = jnp.broadcast_to(wide[:, None, :], (line, 8, 128))
    return (row == column), [jnp.where(spread == g, 1.0, 0.0) for g in range(groups)]


def mixing(linked, rank):
    line = linked.shape[0]
    size = line * rank
    owner = lax.broadcasted_iota(jnp.int32, (size, line), 0) // rank
    block = lax.broadcasted_iota(jnp.int32, (size, line), 1)
    spread = jnp.where(owner == block, 1.0, 0.0).astype(BF16)
    tall = jnp.dot(spread, linked.astype(BF16), preferred_element_type=F32).astype(BF16)
    big = lax.dot_general(tall, spread, (((1,), (1,)), ((), ())), preferred_element_type=F32)
    rows = lax.broadcasted_iota(jnp.int32, (size, size), 0)
    across = lax.broadcasted_iota(jnp.int32, (size, size), 1)
    return jnp.where(rows % rank == across % rank, big, 0.0).astype(BF16)


def whole_kernel(
    groups, group_cols,
    acts_ref, init_ref, kept_ref, member_ref,
    bases_ref, latent_ref,
    full_ref, image_all, gram_ref, basis_ref, init_v, init_out, init_in,
    proj_out, proj_in, mixed_out, mixed_in, part_out, part_in, sum_out, sum_in,
    m_ref, w_ref, mix_ref, codes_out, codes_in, turned,
    local_sems, sems, xs, xr, is_, ir,
):
    here = Place()
    line, tok = here.line, here.tok
    rows = init_v.shape[0]
    rank, cols = basis_ref.shape
    total_rank = rank * tok
    tokens = line * proj_out.shape[2]
    reducers, per_tile = part_out.shape[:2]

    acts_copy = pltpu.make_async_copy(acts_ref, turned_acts(full_ref, here), local_sems.at[0])
    init_copy = pltpu.make_async_copy(init_ref, init_v, local_sems.at[1])
    acts_copy.start()
    init_copy.start()
    greet_start(line_devices(here) + plane_devices(here))
    init_copy.wait()
    turned_init = init_v[...].T
    if tok > 1:
        wide = jnp.concatenate([turned_init, jnp.zeros((total_rank, 128 - rows), F32)], axis=1)
        init_out[...] = wide.astype(BF16).reshape(init_out.shape)
    else:
        basis_ref[...] = turned_init.astype(BF16)
    acts_copy.wait()
    greet_finish(line + tok - 2)

    plane_gather_start(here, full_ref, xs, xr)
    spread = Exchange(here.p, tok, here.in_plane, init_out, init_in, sems, 0)
    if tok > 1:
        spread.send_all()
        spread.keep()
    same, member_masks = masks(member_ref, line, groups)
    linked = jnp.where(same, kept_ref[...].astype(F32), 0.0)
    mix_ref[...] = mixing(linked, rank)
    plane_gather_finish(here, full_ref, xs, xr)
    if tok > 1:
        spread.received()
        spread.sent()
        per = 128 // rows
        for c in range(tok // per):
            total = init_in[c * per].astype(F32)
            for d in range(1, per):
                total += pltpu.roll(init_in[c * per + d].astype(F32), d * rows, 1)
            basis_ref[:, c * 128 : c * 128 + 128] = total.astype(BF16)
    plane_gather_sent(here, full_ref, xs, xr)

    chunk = tokens // line
    per_step = 2 if line % 2 == 0 else 1
    steps = line // per_step
    proj_x = Exchange(here.k, line, here.in_line, proj_out, proj_in, sems, 1)
    mixed_x = Exchange(here.k, line, here.in_line, mixed_out, mixed_in, sems, 2)
    part_x = Exchange(here.k, line, here.in_line, part_out, part_in, sems, 3)
    sum_x = Exchange(here.k, line, here.in_line, sum_out, sum_in, sems, 4)
    gram_x = Exchange(here.p, tok, here.in_plane, gram_ref, gram_ref, sems, 5)
    codes_x = Exchange(here.k, line, here.in_line, codes_out, codes_in, sems, 6)
    reducing = here.k < reducers

    def iteration(turn, carry):
        image_ref = image_all.at[turn]

        def project(d, carry):
            u = (here.k // per_step + 1 + d) % steps
            proj = lax.dot_general(
                basis_ref[...], tokens_at(full_ref, u, per_step * chunk),
                (((1,), (1,)), ((), ())), preferred_element_type=F32,
            ).astype(BF16)
            for v in range(per_step):
                c = u * per_step + v
                proj_out[c] = proj[:, v * chunk : (v + 1) * chunk]

                @pl.when(c != here.k)
                def _():
                    proj_x.send(c)

            return carry

        lax.fori_loop(0, steps, project, 0)
        proj_x.keep()
        proj_x.received()
        stacked = proj_in[...].reshape(line * rank, chunk)
        mixed_out[...] = (
            jnp.dot(mix_ref[...], stacked, preferred_element_type=F32)
            .astype(BF16)
            .reshape(mixed_out.shape)
        )
        mixed_x.send_all()
        mixed_x.keep()
        mixed_x.received()
        mixed = jnp.concatenate([mixed_in[c] for c in range(line)], axis=1)
        acts = full_ref[...].reshape(tokens, cols)
        image = jnp.dot(mixed, acts, preferred_element_type=F32)
        image = image * (1.0 / tokens) + RIDGE * basis_ref[...].astype(F32)
        image_ref[here.y, here.x] = image.reshape(image_ref.shape[2:])
        plane_gather_start(here, image_ref, is_, ir)
        plane_gather_finish(here, image_ref, is_, ir)

        whole = image_ref[...].reshape(total_rank, cols)
        tiles = []
        for c in range(0, total_rank, LEAF):
            high = (total_rank - c) // tok
            mine = [eight_rows(image_ref, c + here.p * high + r) for r in range(0, high, 8)]
            tile = dot_t(jnp.concatenate(mine, axis=0), whole[c : c + LEAF])
            tiles.append(tile.reshape(high // 8, 8, LEAF))
        part_out[...] = jnp.concatenate(tiles, axis=0).reshape(part_out.shape)

        def send_part(d, carry):
            to = lax.rem(here.k + d, line)

            @pl.when(to < reducers)
            def _():
                part_x.send(to)

            return carry

        lax.fori_loop(1, line, send_part, 0)

        @pl.when(reducing)
        def _():
            part_x.keep()
            part_x.received()
            totals = [
                jnp.sum(part_in[...] * mask[:, None], axis=0) for mask in member_masks
            ]
            for i in range(line):
                mine = member_masks[0][i][None] * totals[0]
                for g in range(1, groups):
                    mine += member_masks[g][i][None] * totals[g]
                sum_out[i] = mine
            sum_x.send_all()
            sum_x.keep()
            sum_x.received(reducers - 1)

        @pl.when(jnp.logical_not(reducing))
        def _():
            sum_x.received(reducers)

        gram_ref[here.p] = sum_in[...].reshape(gram_ref.shape[1:])
        if tok > 1:
            def send_gram(d, carry):
                to = lax.rem(here.p + d, tok)
                mine = gram_ref.at[here.p]
                group_copy(mine, mine, sems, 5, here.in_plane(to)).start()
                return carry

            lax.fori_loop(1, tok, send_gram, 0)
            gram_x.received()
        first = 0
        for c in range(0, total_rank, LEAF):
            count = (total_rank - c) // tok // 8
            panel = gram_ref[:, first : first + count].reshape(total_rank - c, LEAF)
            m_ref[c:, c : c + LEAF] = panel * (1.0 / group_cols)
            first += count

        proj_x.sent()
        mixed_x.sent()
        plane_gather_sent(here, image_ref, is_, ir)

        @pl.when(reducing)
        def _():
            part_x.sent(reducers - 1)
            sum_x.sent()

        @pl.when(jnp.logical_not(reducing))
        def _():
            part_x.sent(reducers)

        if tok > 1:
            gram_x.sent()
        factor_inverse(m_ref, w_ref)

        @pl.when(turn < ITERS - 1)
        def _():
            at = pl.multiple_of(here.p * rank, rank)
            image = image_ref[...].reshape(total_rank, cols)
            basis_ref[...] = dot(w_ref[pl.ds(at, rank), :], image).astype(BF16)

        return carry

    lax.fori_loop(0, ITERS, iteration, 0)

    image = image_all[ITERS - 1].reshape(total_rank, cols)
    basis = dot(w_ref[...], image).astype(BF16)
    own = full_ref[here.y, here.x].reshape(tokens // tok, cols)
    codes = lax.dot_general(own, basis, (((1,), (1,)), ((), ())), preferred_element_type=F32)
    codes_out[...] = codes.reshape(codes_out.shape)
    codes_x.send_all()
    codes_x.keep()
    wide = turned.shape[0]
    per = wide // rows
    at = pl.multiple_of(here.p // per * wide, wide)
    part = image_all[ITERS - 1, :, :, :, :, pl.ds(at, wide)].reshape(total_rank, wide)
    turned[...] = dot(w_ref[...], part).T
    bases_ref[...] = turned[pl.ds(pl.multiple_of(here.p % per * rows, rows), rows), :]
    codes_x.received()
    scale = 1.0 / math.sqrt(group_cols)
    for g in range(groups):
        for c in range(0, total_rank, 128):
            total = jnp.sum(codes_in[:, :, c : c + 128] * member_masks[g][:, :1], axis=0)
            latent_ref[:, g * total_rank + c : g * total_rank + c + 128] = (total * scale).astype(BF16)
    codes_x.sent()


def turned_acts(full_ref, here):
    return full_ref.at[here.y, here.x]


def greet_start(devices):
    barrier = pltpu.get_barrier_semaphore()
    for device in devices:
        pl.semaphore_signal(barrier, inc=1, device_id=device, device_id_type=MESH)


def greet_finish(count):
    pl.semaphore_wait(pltpu.get_barrier_semaphore(), count)


def per_device(acts, init_basis, kept, member):
    tok = lax.axis_size("tok")
    line = lax.axis_size("gr") * lax.axis_size("gc")
    side = math.isqrt(tok)
    groups = kept.shape[0] // GBLK
    rows, total_rank = init_basis.shape[1:]
    shard, cols = acts.shape
    tokens = shard * tok
    rank = total_rank // tok
    group_cols = GBLK * rows * tok
    tiles = sum((total_rank - c) // tok // 8 for c in range(0, total_rank, LEAF))
    reducers = max(d for d in range(1, line + 1) if tiles % d == 0)
    per_tile = tiles // reducers
    pieces = (line, rank, tokens // line)
    init_pieces = (tok, rank, 128)
    codes = (line, shard // line, total_rank)
    bases, latent = pl.pallas_call(
        functools.partial(whole_kernel, groups, group_cols),
        out_shape=(
            jax.ShapeDtypeStruct((rows, total_rank), F32),
            jax.ShapeDtypeStruct((shard // line, groups * total_rank), BF16),
        ),
        in_specs=[pl.BlockSpec(memory_space=pl.ANY), pl.BlockSpec(memory_space=pl.ANY), vmem(), vmem()],
        out_specs=(vmem(), vmem()),
        scratch_shapes=[
            pltpu.VMEM((side, side, 4, shard // 4, cols), BF16),
            pltpu.VMEM((ITERS, side, side, 4, rank // 4, cols), F32),
            pltpu.VMEM((tok, tiles, 8, LEAF), F32),
            pltpu.VMEM((rank, cols), BF16),
            pltpu.VMEM((rows, total_rank), F32),
            pltpu.VMEM(init_pieces, BF16),
            pltpu.VMEM(init_pieces, BF16),
            pltpu.VMEM(pieces, BF16),
            pltpu.VMEM(pieces, BF16),
            pltpu.VMEM(pieces, BF16),
            pltpu.VMEM(pieces, BF16),
            pltpu.VMEM((reducers, per_tile, 8, LEAF), F32),
            pltpu.VMEM((line, per_tile, 8, LEAF), F32),
            pltpu.VMEM((line, per_tile, 8, LEAF), F32),
            pltpu.VMEM((reducers, per_tile, 8, LEAF), F32),
            pltpu.VMEM((total_rank, total_rank), F32),
            pltpu.VMEM((total_rank, total_rank), F32),
            pltpu.VMEM((line * rank, line * rank), BF16),
            pltpu.VMEM(codes, F32),
            pltpu.VMEM(codes, F32),
            pltpu.VMEM((max(rows, 128), total_rank), F32),
            pltpu.SemaphoreType.DMA((2,)),
            pltpu.SemaphoreType.DMA((2, 7)),
            pltpu.SemaphoreType.DMA((4, 6)),
            pltpu.SemaphoreType.DMA((4, 6)),
            pltpu.SemaphoreType.DMA((4, 6)),
            pltpu.SemaphoreType.DMA((4, 6)),
        ],
        compiler_params=params(0),
    )(acts.reshape(4, shard // 4, cols), init_basis[0], kept, member.reshape(1, -1))
    return bases[None], latent


def solution(mesh):
    placed = (P("tok", ("gr", "gc")), P(("gr", "gc"), "tok", None), P(), P())
    return jax.shard_map(
        per_device,
        mesh=mesh,
        in_specs=placed,
        out_specs=(P(("gr", "gc"), "tok", None), P(("tok", "gr", "gc"), None)),
        check_vma=False,
    )
```

time: 1530 us -> 208 us (0.14)
  waiting for transfers between devices: 993 us -> 0 us
  other arithmetic: 421 us -> 0 us
  Pallas kernels: 0 us -> 202 us
  matrix products: 45.2 us -> 0 us
  local copies, waits for them, and re-layouts: 44.4 us -> 4.46 us
    psum x2 -> x0, waiting for transfers between devices: 520 us -> none  [per_device(): gram = lax.psum(stacked, ('tok', 'gr', 'gc'))]
    another operation x41 -> x0, other arithmetic: 400 us -> none  [the longest x32 319 us: per_device(): lower = jnp.linalg.cholesky(gram / group_cols)]
    all_gather x5 -> x0, waiting for transfers between devices: 226 us -> none  [the longest x3 146 us: full_rows(): lax.all_gather(basis_slice.astype(jnp.bfloat16), 'tok', axis=1, tiled=True)]
    pallas_call x0 -> x1, Pallas kernels: none -> 202 us  [per_device(): pl.pallas_call(functools.partial(whole_kernel, groups, group_cols), out_s...]
    unnamed x12 -> x0, waiting for transfers between devices: 193 us -> none
    reduce_scatter x1 -> x0, waiting for transfers between devices: 53.7 us -> none  [per_device(): lax.psum_scatter(placed.reshape(tok_rows // lax.axis_size(('gr', 'gc')) *...]
    dot_general x11 -> x0, matrix products: 24.9 us -> none  [the longest x2 10.5 us: per_device(): own_lower = jnp.einsum('og,grs->ors', selector, lower, precision=highest)]
    another operation x26 -> x0, matrix products: 20.3 us -> none  [the longest x12 17.1 us: per_device(): lower = jnp.linalg.cholesky(gram / group_cols)]
  transfers between devices with their start and end apart: 10 -> 0, of which waited for: 10 -> 0; matrix products, arithmetic and copies ran while one was open for 0% -> 0% of each run, Pallas kernels for 0% -> 0%
where the time goes in v2:
time: 208 us; the launch traced here: 207 us
  Pallas kernels  202 us (97%)
  local copies, waits for them, and re-layouts  4.46 us (2%)
    pallas_call x1, Pallas kernels, per_device(): pl.pallas_call(functools.partial(whole_kernel, groups, group_cols), out_s...  202 us
    unnamed x10, local copies, waits for them, and re-layouts  4.46 us

profile of v2, /device:TPU:1, one launch (start us, length us, event | category | flops | bytes accessed | tf_op | source)
XLA Modules:
  0.0 207.4 jit_solution(12380508686104504395)
XLA Ops:
  0.6 0.0 copy-start.3
  0.6 0.6 copy-done.3
  1.3 0.0 copy-start
  1.3 0.9 copy-done
  2.2 0.0 copy-start.1
  2.2 0.9 copy-done.1
  3.1 0.0 copy-start.2
  3.1 0.7 copy-done.2
  3.8 202.3 %shard_map.59 = (f32[64,512]{1,0:T(8,128)S(1)}, bf16[8,1024]{1,0:T(8,128)(2,1)S(1)}) custom-call(bf16[4,32,1024]{2,1,0:T(8,128)(2,1)S(1)} %bitcast.4, f32[64,512]{1,0:T(8,128)S(1)} %bitcast.5, s32[16,16]{1,0:T(8,128)S(1)} %copy-done.2, s32[1,16]{1,0:T(1,128)S(1)} %bitcast.7), custom_call_target="tpu_custom_call" | custom-call | tf_op jit(solution)/shard_map/pallas_call | solution.py:585
  206.2 0.7 copy.8
  206.8 0.6 copy.9
Async XLA Ops:
  0.6 0.7 copy-start.3
  1.3 0.9 copy-start
  2.2 0.9 copy-start.1
  3.1 0.7 copy-start.2

commit v3 on v2

--- a/solution.py
+++ b/solution.py
@@ -12,9 +12,10 @@
 ITERS = 2
 RIDGE = 2.0
 LEAF = 128
+HIGH = 16
 MESH = pl.DeviceIdType.MESH
 HIGHEST = lax.Precision.HIGHEST
-VMEM_LIMIT = 48 * 2**20
+VMEM_LIMIT = 60 * 2**20
 F32 = jnp.float32
 BF16 = jnp.bfloat16
 
@@ -93,83 +94,83 @@
     )
 
 
-class Ring:
-    def __init__(self, here, axis, piece, send, recv):
-        at = here.x if axis == "x" else here.y
-        side = here.side
-        self.me, self.right, self.left = at, (at + 1) % side, (at + side - 1) % side
-        self.opp = (at + 2) % side
-        self.to_right = here.at_axis(axis, self.right)
-        self.to_left = here.at_axis(axis, self.left)
-        self.piece, self.send, self.recv = piece, send, recv
-
-    def copy(self, slot, owner, part, device):
-        ref = self.piece(owner, part)
-        return rcopy(ref, ref, self.send.at[slot], self.recv.at[slot], device)
+class Gather:
+    PARTS = ((0, 2), (0, 2), (0, 1), (1, 1))
+
+    def __init__(self, here, buf, send, recv):
+        self.here, self.buf, self.send, self.recv = here, buf, send, recv
+        self.side = here.side
+        self.axes = (("x", "y"), ("y", "x"))
+        self.at = ((here.x, here.y), (here.y, here.x))
+
+    def near(self, part, ring, step):
+        return lax.rem(self.at[part][ring] + step, self.side)
+
+    def copy(self, part, ring, kind, owner, rel, slot):
+        low, number = self.PARTS[kind]
+        first, second = (owner, self.at[part][1]) if ring == 0 else (self.near(part, 0, rel), owner)
+        y, x = (second, first) if part == 0 else (first, second)
+        ref = self.buf.at[y, x, pl.ds(2 * part + low, number)]
+        to = self.near(part, ring, 1 if kind in (0, 2) else self.side - 1)
+        device = self.here.at_axis(self.axes[part][ring], to)
+        return rcopy(ref, ref, self.send.at[ring], self.recv.at[part, slot], device)
+
+    def one(self, part, kind, step):
+        return self.copy(part, 0, kind, self.near(part, 0, step), 0, kind)
+
+    def two(self, part, rel, kind, step):
+        return self.copy(part, 1, kind, self.near(part, 1, step), rel, 4 + 4 * rel + kind)
 
     def start(self):
-        self.copy(0, self.me, 0, self.to_right).start()
-        self.copy(1, self.me, 1, self.to_left).start()
-        self.copy(2, self.me, 1, self.to_right).start()
-        self.copy(3, self.me, 0, self.to_left).start()
-
-    def forward(self):
-        self.copy(0, self.left, 0, self.to_right).wait_recv()
-        self.copy(4, self.left, 0, self.to_right).start()
-        self.copy(1, self.right, 1, self.to_left).wait_recv()
-        self.copy(5, self.right, 1, self.to_left).start()
+        if self.here.tok == 1:
+            return
+        for part in (0, 1):
+            self.one(part, 0, 0).start()
+            self.one(part, 1, 0).start()
+        for part in (0, 1):
+            self.share(part, 0)
+
+    def share(self, part, rel):
+        self.two(part, rel, 0, 0).start()
+        self.two(part, rel, 1, 0).start()
+
+    def pass_on(self, part, rel):
+        self.two(part, rel, 0, 3).wait_recv()
+        self.two(part, rel, 2, 3).start()
+        self.two(part, rel, 1, 1).wait_recv()
+        self.two(part, rel, 3, 1).start()
 
     def finish(self):
-        self.copy(2, self.left, 1, self.to_right).wait_recv()
-        self.copy(3, self.right, 0, self.to_left).wait_recv()
-        self.copy(4, self.opp, 0, self.to_right).wait_recv()
-        self.copy(5, self.opp, 1, self.to_left).wait_recv()
+        if self.here.tok == 1:
+            return
+        for part in (0, 1):
+            self.one(part, 0, 3).wait_recv()
+            self.one(part, 2, 3).start()
+            self.share(part, 3)
+        for part in (0, 1):
+            self.one(part, 1, 1).wait_recv()
+            self.one(part, 3, 1).start()
+            self.share(part, 1)
+        for part in (0, 1):
+            self.pass_on(part, 0)
+        for part in (0, 1):
+            self.one(part, 2, 2).wait_recv()
+            self.one(part, 3, 2).wait_recv()
+            self.share(part, 2)
+        for rel in (3, 1, 2):
+            for part in (0, 1):
+                self.pass_on(part, rel)
+        for rel in (0, 3, 1, 2):
+            for part in (0, 1):
+                self.two(part, rel, 2, 2).wait_recv()
+                self.two(part, rel, 3, 2).wait_recv()
 
     def sent(self):
-        self.copy(0, self.me, 0, self.to_right).wait_send()
-        self.copy(1, self.me, 1, self.to_left).wait_send()
-        self.copy(2, self.me, 1, self.to_right).wait_send()
-        self.copy(3, self.me, 0, self.to_left).wait_send()
-        self.copy(4, self.left, 0, self.to_right).wait_send()
-        self.copy(5, self.right, 1, self.to_left).wait_send()
-
-
-def plane_rings(here, buf, send, recv):
-    y, x = here.y, here.x
-    return (
-        Ring(here, "x", lambda at, part: buf.at[y, at, part], send.at[0], recv.at[0]),
-        Ring(here, "y", lambda at, part: buf.at[at, x, 2 + part], send.at[1], recv.at[1]),
-        Ring(here, "y", lambda at, part: buf.at[at, :, part], send.at[2], recv.at[2]),
-        Ring(here, "x", lambda at, part: buf.at[:, at, 2 + part], send.at[3], recv.at[3]),
-    )
-
-
-def plane_gather_start(here, buf, send, recv):
-    if here.tok > 1:
-        one_a, one_b, _, _ = plane_rings(here, buf, send, recv)
-        one_a.start()
-        one_b.start()
-
-
-def plane_gather_finish(here, buf, send, recv):
-    if here.tok > 1:
-        one_a, one_b, two_a, two_b = plane_rings(here, buf, send, recv)
-        one_a.forward()
-        one_b.forward()
-        one_a.finish()
-        two_a.start()
-        one_b.finish()
-        two_b.start()
-        two_a.forward()
-        two_b.forward()
-        two_a.finish()
-        two_b.finish()
-
-
-def plane_gather_sent(here, buf, send, recv):
-    if here.tok > 1:
-        for ring in plane_rings(here, buf, send, recv):
-            ring.sent()
+        if self.here.tok == 1:
+            return
+        device = self.here.at_axis("x", self.near(0, 0, 1))
+        for ring, ref in ((0, self.buf.at[0, pl.ds(0, 3)]), (1, self.buf.at[pl.ds(0, 3)])):
+            rcopy(ref, ref, self.send.at[ring], self.recv.at[0, 0], device).wait_send()
 
 
 def group_copy(src, dst, sems, which, device):
@@ -214,8 +215,8 @@
 
 
 def leaf_inverse(block):
-    count, high, wide = block.shape
-    shape = (high, wide)
+    count = LEAF // HIGH
+    shape = (HIGH, LEAF)
     lane = lax.broadcasted_iota(jnp.int32, shape, 1)
     sub = lax.broadcasted_iota(jnp.int32, shape, 0)
 
@@ -223,37 +224,37 @@
         return jnp.broadcast_to(v[r : r + 1, :], shape)
 
     done = []
-    rest = block
+    rest = block.reshape(count, HIGH, LEAF)
     for s in range(count):
-        c0 = 8 * s
+        c0 = HIGH * s
         here = rest[0]
-        cols = [jnp.broadcast_to(here[:, c0 + j : c0 + j + 1], shape) for j in range(8)]
-        diag = (lane >= c0) & (lane < c0 + 8)
+        cols = [jnp.broadcast_to(here[:, c0 + j : c0 + j + 1], shape) for j in range(HIGH)]
+        diag = (lane >= c0) & (lane < c0 + HIGH)
         first = jnp.where(diag, jnp.where(lane - c0 == sub, 1.0, 0.0), here)
         full, low = first, first
         pivots = jnp.ones(shape, F32)
-        for j in range(8):
+        for j in range(HIGH):
             pivot = down(cols[j], j)
             inverse = 1.0 / pivot
             others = jnp.where(sub == j, 0.0, cols[j])
             below = jnp.where(sub > j, cols[j], 0.0)
-            for k in range(j + 1, 8):
+            for k in range(j + 1, HIGH):
                 cols[k] = cols[k] - (others * down(cols[k], j)) * inverse
             full = full - (others * down(full, j)) * inverse
             low = low - (below * down(low, j)) * inverse
             pivots = jnp.where(sub == j, pivot, pivots)
         solved = full / pivots
-        done.append(jnp.where(lane < c0 + 8, low * lax.rsqrt(pivots), 0.0))
+        done.append(jnp.where(lane < c0 + HIGH, low * lax.rsqrt(pivots), 0.0))
         if s + 1 < count:
             old = rest[1:]
             terms = [
                 jnp.broadcast_to(old[:, :, c0 + k : c0 + k + 1], old.shape) * down(solved, k)[None]
-                for k in range(8)
+                for k in range(HIGH)
             ]
             while len(terms) > 1:
                 terms = [terms[i] + terms[i + 1] for i in range(0, len(terms), 2)]
             rest = jnp.where(diag[None], 0.0, old) - terms[0]
-    return jnp.stack(done)
+    return jnp.stack(done).reshape(LEAF, LEAF)
 
 
 def dot(a, b):
@@ -272,7 +273,7 @@
 
     def turn(step, carry):
         at = pl.ds(pl.multiple_of(step * LEAF, LEAF), LEAF)
-        w_ref[at, at] = leaf_inverse(m_ref[at, at].reshape(LEAF // 8, 8, LEAF)).reshape(LEAF, LEAF)
+        w_ref[at, at] = leaf_inverse(m_ref[at, at])
         for b in range(size // LEAF):
             r0, r1 = b * LEAF, (b + 1) * LEAF
 
@@ -350,7 +351,7 @@
     bases_ref, latent_ref,
     full_ref, image_all, gram_ref, basis_ref, init_v, init_out, init_in,
     proj_out, proj_in, mixed_out, mixed_in, part_out, part_in, sum_out, sum_in,
-    m_ref, w_ref, mix_ref, codes_out, codes_in, turned,
+    m_ref, w_ref, mix_ref, codes_out, codes_in, mapped, turned,
     local_sems, sems, xs, xr, is_, ir,
 ):
     here = Place()
@@ -376,7 +377,8 @@
     acts_copy.wait()
     greet_finish(line + tok - 2)
 
-    plane_gather_start(here, full_ref, xs, xr)
+    acts_x = Gather(here, full_ref, xs, xr)
+    acts_x.start()
     spread = Exchange(here.p, tok, here.in_plane, init_out, init_in, sems, 0)
     if tok > 1:
         spread.send_all()
@@ -384,7 +386,7 @@
     same, member_masks = masks(member_ref, line, groups)
     linked = jnp.where(same, kept_ref[...].astype(F32), 0.0)
     mix_ref[...] = mixing(linked, rank)
-    plane_gather_finish(here, full_ref, xs, xr)
+    acts_x.finish()
     if tok > 1:
         spread.received()
         spread.sent()
@@ -394,7 +396,7 @@
             for d in range(1, per):
                 total += pltpu.roll(init_in[c * per + d].astype(F32), d * rows, 1)
             basis_ref[:, c * 128 : c * 128 + 128] = total.astype(BF16)
-    plane_gather_sent(here, full_ref, xs, xr)
+    acts_x.sent()
 
     chunk = tokens // line
     per_step = 2 if line % 2 == 0 else 1
@@ -443,8 +445,9 @@
         image = jnp.dot(mixed, acts, preferred_element_type=F32)
         image = image * (1.0 / tokens) + RIDGE * basis_ref[...].astype(F32)
         image_ref[here.y, here.x] = image.reshape(image_ref.shape[2:])
-        plane_gather_start(here, image_ref, is_, ir)
-        plane_gather_finish(here, image_ref, is_, ir)
+        image_x = Gather(here, image_ref, is_, ir)
+        image_x.start()
+        image_x.finish()
 
         whole = image_ref[...].reshape(total_rank, cols)
         tiles = []
@@ -465,6 +468,11 @@
             return carry
 
         lax.fori_loop(1, line, send_part, 0)
+
+        @pl.when(turn == ITERS - 1)
+        def _():
+            own = full_ref[here.y, here.x].reshape(tokens // tok, cols).astype(F32)
+            mapped[...] = dot_t(own, image_ref[...].reshape(total_rank, cols))
 
         @pl.when(reducing)
         def _():
@@ -505,7 +513,7 @@
 
         proj_x.sent()
         mixed_x.sent()
-        plane_gather_sent(here, image_ref, is_, ir)
+        image_x.sent()
 
         @pl.when(reducing)
         def _():
@@ -530,11 +538,9 @@
 
     lax.fori_loop(0, ITERS, iteration, 0)
 
-    image = image_all[ITERS - 1].reshape(total_rank, cols)
-    basis = dot(w_ref[...], image).astype(BF16)
-    own = full_ref[here.y, here.x].reshape(tokens // tok, cols)
-    codes = lax.dot_general(own, basis, (((1,), (1,)), ((), ())), preferred_element_type=F32)
-    codes_out[...] = codes.reshape(codes_out.shape)
+    codes = dot_t(mapped[...], w_ref[...]).reshape(line, -1, total_rank)
+    half = total_rank // 2
+    codes_out[...] = jnp.concatenate([codes[:, :, :half], codes[:, :, half:]], axis=1).astype(BF16)
     codes_x.send_all()
     codes_x.keep()
     wide = turned.shape[0]
@@ -545,10 +551,15 @@
     bases_ref[...] = turned[pl.ds(pl.multiple_of(here.p % per * rows, rows), rows), :]
     codes_x.received()
     scale = 1.0 / math.sqrt(group_cols)
+    few = latent_ref.shape[0]
     for g in range(groups):
-        for c in range(0, total_rank, 128):
-            total = jnp.sum(codes_in[:, :, c : c + 128] * member_masks[g][:, :1], axis=0)
-            latent_ref[:, g * total_rank + c : g * total_rank + c + 128] = (total * scale).astype(BF16)
+        for c in range(0, half, 128 if half % 128 == 0 else half):
+            size = min(128, half)
+            mask = member_masks[g][:, :1, :size]
+            total = jnp.sum(codes_in[:, :, c : c + size].astype(F32) * mask, axis=0) * scale
+            for h in (0, 1):
+                at = g * total_rank + h * half + c
+                latent_ref[:, at : at + size] = total[h * few : (h + 1) * few].astype(BF16)
     codes_x.sent()
 
 
@@ -581,7 +592,7 @@
     per_tile = tiles // reducers
     pieces = (line, rank, tokens // line)
     init_pieces = (tok, rank, 128)
-    codes = (line, shard // line, total_rank)
+    codes = (line, shard // line * 2, total_rank // 2)
     bases, latent = pl.pallas_call(
         functools.partial(whole_kernel, groups, group_cols),
         out_shape=(
@@ -609,15 +620,16 @@
             pltpu.VMEM((total_rank, total_rank), F32),
             pltpu.VMEM((total_rank, total_rank), F32),
             pltpu.VMEM((line * rank, line * rank), BF16),
-            pltpu.VMEM(codes, F32),
-            pltpu.VMEM(codes, F32),
+            pltpu.VMEM(codes, BF16),
+            pltpu.VMEM(codes, BF16),
+            pltpu.VMEM((shard, total_rank), F32),
             pltpu.VMEM((max(rows, 128), total_rank), F32),
             pltpu.SemaphoreType.DMA((2,)),
             pltpu.SemaphoreType.DMA((2, 7)),
-            pltpu.SemaphoreType.DMA((4, 6)),
-            pltpu.SemaphoreType.DMA((4, 6)),
-            pltpu.SemaphoreType.DMA((4, 6)),
-            pltpu.SemaphoreType.DMA((4, 6)),
+            pltpu.SemaphoreType.DMA((2,)),
+            pltpu.SemaphoreType.DMA((2, 20)),
+            pltpu.SemaphoreType.DMA((2,)),
+            pltpu.SemaphoreType.DMA((2, 20)),
         ],
         compiler_params=params(0),
     )(acts.reshape(4, shard // 4, cols), init_basis[0], kept, member.reshape(1, -1))

time: 208 us -> 189 us (0.909)
  Pallas kernels: 202 us -> 186 us
  local copies, waits for them, and re-layouts: 4.46 us -> 2.18 us
    pallas_call x1, Pallas kernels: 202 us -> 186 us  [per_device(): pl.pallas_call(functools.partial(whole_kernel, groups, group_cols), out_s...]
    unnamed x10 -> x4, local copies, waits for them, and re-layouts: 4.46 us -> 2.18 us
where the time goes in v3:
time: 189 us
  Pallas kernels  186 us (98%)
  local copies, waits for them, and re-layouts  2.18 us (1%)
    pallas_call x1, Pallas kernels, per_device(): pl.pallas_call(functools.partial(whole_kernel, groups, group_cols), out_s...  186 us

profile of v3, /device:TPU:1, one launch (start us, length us, event | category | flops | bytes accessed | tf_op | source)
XLA Modules:
  0.0 189.2 jit_solution(8345785720751972323)
XLA Ops:
  0.6 186.4 %shard_map.59 = (f32[64,512]{1,0:T(8,128)}, bf16[8,1024]{1,0:T(8,128)(2,1)}) custom-call(bf16[4,32,1024]{2,1,0:T(8,128)(2,1)} %bitcast.4, f32[64,512]{1,0:T(8,128)} %bitcast.5, s32[16,16]{1,0:T(8,128)} %kept_ref.1, s32[1,16]{1,0:T(1,128)} %bitcast.7), custom_call_target="tpu_custom_call" | custom-call | tf_op jit(solution)/shard_map/pallas_call | solution.py:596
  187.0 0.0 copy-start
  187.0 1.6 copy.8
  188.6 0.0 copy-done
  188.6 0.6 copy.9
Async XLA Ops:
  187.0 1.6 copy-start

commit v4 on v3

--- a/solution.py
+++ b/solution.py
@@ -171,6 +171,55 @@
         device = self.here.at_axis("x", self.near(0, 0, 1))
         for ring, ref in ((0, self.buf.at[0, pl.ds(0, 3)]), (1, self.buf.at[pl.ds(0, 3)])):
             rcopy(ref, ref, self.send.at[ring], self.recv.at[0, 0], device).wait_send()
+
+
+class Cross:
+    def __init__(self, here, buf, sems):
+        self.here, self.buf, self.sems = here, buf, sems
+        self.side = here.side
+        self.axes = (("x", "y"), ("y", "x"))
+        self.at = ((here.x, here.y), (here.y, here.x))
+
+    def go(self, part, ring, rel):
+        first = lax.rem(self.at[part][0] + rel, self.side)
+        second = self.at[part][1]
+        y, x = (second, first) if part == 0 else (first, second)
+        ref = self.buf.at[y, x, pl.ds(2 * part, 2)]
+        which = 2 * part + ring
+        for d in (2, 1, 3):
+            to = lax.rem(self.at[part][ring] + d, self.side)
+            device = self.here.at_axis(self.axes[part][ring], to)
+            rcopy(ref, ref, self.sems.at[0, which], self.sems.at[1, which], device).start()
+
+    def whole(self, part, ring):
+        ref = self.buf.at[0, pl.ds(0, 3), pl.ds(0, 2)] if ring == 0 else self.buf.at[pl.ds(0, 3), :, pl.ds(0, 2)]
+        which = 2 * part + ring
+        device = self.here.at_axis("x", lax.rem(self.here.x + 1, self.side))
+        return rcopy(ref, ref, self.sems.at[0, which], self.sems.at[1, which], device)
+
+    def start(self):
+        if self.here.tok > 1:
+            for ring in (0, 1):
+                for part in (0, 1):
+                    self.go(part, ring, 0)
+
+    def middle(self):
+        if self.here.tok > 1:
+            for part in (0, 1):
+                self.whole(part, 0).wait_recv()
+                for rel in (1, 3, 2):
+                    self.go(part, 1, rel)
+
+    def finish(self):
+        if self.here.tok > 1:
+            for part in (0, 1):
+                self.whole(part, 1).wait_recv()
+
+    def sent(self):
+        if self.here.tok > 1:
+            for part in (0, 1):
+                for ring in (0, 1):
+                    self.whole(part, ring).wait_send()
 
 
 def group_copy(src, dst, sems, which, device):
@@ -322,6 +371,18 @@
     return image_ref[(*place, pl.ds(pl.multiple_of(within % quarter, 8), 8))]
 
 
+def thirds(x, axis=0):
+    high = x.astype(BF16)
+    rest = x - high.astype(F32)
+    middle = rest.astype(BF16)
+    return jnp.concatenate([high, middle, (rest - middle.astype(F32)).astype(BF16)], axis=axis)
+
+
+def sum_thirds(x, axis=0):
+    high, middle, low = jnp.split(x, 3, axis=axis)
+    return high + (middle + low)
+
+
 def masks(member_ref, line, groups):
     rows = lax.broadcasted_iota(jnp.int32, (line, line), 0)
     across = lax.broadcasted_iota(jnp.int32, (line, line), 1)
@@ -351,8 +412,9 @@
     bases_ref, latent_ref,
     full_ref, image_all, gram_ref, basis_ref, init_v, init_out, init_in,
     proj_out, proj_in, mixed_out, mixed_in, part_out, part_in, sum_out, sum_in,
+    wide_out, wide_in, summed_out, summed_in, thirds_ref,
     m_ref, w_ref, mix_ref, codes_out, codes_in, mapped, turned,
-    local_sems, sems, xs, xr, is_, ir,
+    local_sems, sems, xs, xr, cross_sems,
 ):
     here = Place()
     line, tok = here.line, here.tok
@@ -401,53 +463,72 @@
     chunk = tokens // line
     per_step = 2 if line % 2 == 0 else 1
     steps = line // per_step
-    proj_x = Exchange(here.k, line, here.in_line, proj_out, proj_in, sems, 1)
-    mixed_x = Exchange(here.k, line, here.in_line, mixed_out, mixed_in, sems, 2)
-    part_x = Exchange(here.k, line, here.in_line, part_out, part_in, sems, 3)
-    sum_x = Exchange(here.k, line, here.in_line, sum_out, sum_in, sems, 4)
-    gram_x = Exchange(here.p, tok, here.in_plane, gram_ref, gram_ref, sems, 5)
-    codes_x = Exchange(here.k, line, here.in_line, codes_out, codes_in, sems, 6)
+
+    def line_exchange(src, dst, which):
+        return Exchange(here.k, line, here.in_line, src, dst, sems, which)
+
     reducing = here.k < reducers
+
+    proj_x = line_exchange(proj_out, proj_in, 1)
+    mixed_x = line_exchange(mixed_out, mixed_in, 2)
+    part_x = line_exchange(part_out, part_in, 3)
+    sum_x = line_exchange(sum_out, sum_in, 4)
+    codes_x = line_exchange(codes_out, codes_in, 7)
+    wide_x = line_exchange(wide_out, wide_in, 8)
+    summed_x = line_exchange(summed_out, summed_in, 9)
+    first_image, image, mapped_image = (image_all.at[n] for n in range(3))
+    first_x = Cross(here, first_image, cross_sems.at[0])
+    mapped_x = Cross(here, mapped_image, cross_sems.at[1])
+
+    def project(basis, finish, exchange):
+        def body(d, carry):
+            u = (here.k // per_step + 1 + d) % steps
+            proj = finish(
+                lax.dot_general(
+                    basis[...], tokens_at(full_ref, u, per_step * chunk),
+                    (((1,), (1,)), ((), ())), preferred_element_type=F32,
+                )
+            )
+            for v in range(per_step):
+                c = u * per_step + v
+                exchange.src[c] = proj[:, v * chunk : (v + 1) * chunk]
+
+                @pl.when(c != here.k)
+                def _():
+                    exchange.send(c)
+
+            return carry
+
+        lax.fori_loop(0, steps, body, 0)
+        exchange.keep()
+
+    def acts():
+        return full_ref[...].reshape(tokens, cols)
+
+    project(basis_ref, lambda proj: proj.astype(BF16), proj_x)
+    proj_x.received()
+    stacked = proj_in[...].reshape(line * rank, chunk)
+    mixed_out[...] = (
+        jnp.dot(mix_ref[...], stacked, preferred_element_type=F32)
+        .astype(BF16)
+        .reshape(mixed_out.shape)
+    )
+    mixed_x.send_all()
+    mixed_x.keep()
+    mixed_x.received()
+    mixed = jnp.concatenate([mixed_in[c] for c in range(line)], axis=1)
+    own = jnp.dot(mixed, acts(), preferred_element_type=F32)
+    own = own * (1.0 / tokens) + RIDGE * basis_ref[...].astype(F32)
+    first_image[here.y, here.x] = own.reshape(image_all.shape[3:])
+    first_x.start()
+    thirds_ref[...] = thirds(own)
+    project(thirds_ref, sum_thirds, wide_x)
+    first_x.middle()
+    first_x.finish()
 
     def iteration(turn, carry):
         image_ref = image_all.at[turn]
-
-        def project(d, carry):
-            u = (here.k // per_step + 1 + d) % steps
-            proj = lax.dot_general(
-                basis_ref[...], tokens_at(full_ref, u, per_step * chunk),
-                (((1,), (1,)), ((), ())), preferred_element_type=F32,
-            ).astype(BF16)
-            for v in range(per_step):
-                c = u * per_step + v
-                proj_out[c] = proj[:, v * chunk : (v + 1) * chunk]
-
-                @pl.when(c != here.k)
-                def _():
-                    proj_x.send(c)
-
-            return carry
-
-        lax.fori_loop(0, steps, project, 0)
-        proj_x.keep()
-        proj_x.received()
-        stacked = proj_in[...].reshape(line * rank, chunk)
-        mixed_out[...] = (
-            jnp.dot(mix_ref[...], stacked, preferred_element_type=F32)
-            .astype(BF16)
-            .reshape(mixed_out.shape)
-        )
-        mixed_x.send_all()
-        mixed_x.keep()
-        mixed_x.received()
-        mixed = jnp.concatenate([mixed_in[c] for c in range(line)], axis=1)
-        acts = full_ref[...].reshape(tokens, cols)
-        image = jnp.dot(mixed, acts, preferred_element_type=F32)
-        image = image * (1.0 / tokens) + RIDGE * basis_ref[...].astype(F32)
-        image_ref[here.y, here.x] = image.reshape(image_ref.shape[2:])
-        image_x = Gather(here, image_ref, is_, ir)
-        image_x.start()
-        image_x.finish()
+        gram_at = gram_ref.at[turn]
 
         whole = image_ref[...].reshape(total_rank, cols)
         tiles = []
@@ -468,6 +549,15 @@
             return carry
 
         lax.fori_loop(1, line, send_part, 0)
+
+        @pl.when(turn == 0)
+        def _():
+            wide_x.received()
+            split = thirds(wide_in[...].reshape(line * rank, chunk), axis=1)
+            product = jnp.dot(mix_ref[...], split, preferred_element_type=F32)
+            summed_out[...] = sum_thirds(product, axis=1).reshape(summed_out.shape)
+            summed_x.send_all()
+            summed_x.keep()
 
         @pl.when(turn == ITERS - 1)
         def _():
@@ -494,26 +584,38 @@
         def _():
             sum_x.received(reducers)
 
-        gram_ref[here.p] = sum_in[...].reshape(gram_ref.shape[1:])
+        gram_at[here.p] = sum_in[...].reshape(gram_ref.shape[2:])
+        gram_x = Exchange(here.p, tok, here.in_plane, gram_at, gram_at, sems, 5 + turn)
         if tok > 1:
             def send_gram(d, carry):
                 to = lax.rem(here.p + d, tok)
-                mine = gram_ref.at[here.p]
-                group_copy(mine, mine, sems, 5, here.in_plane(to)).start()
+                mine = gram_at.at[here.p]
+                group_copy(mine, mine, sems, 5 + turn, here.in_plane(to)).start()
                 return carry
 
             lax.fori_loop(1, tok, send_gram, 0)
-            gram_x.received()
+
+        @pl.when(turn == 0)
+        def _():
+            summed_x.received()
+            mixed = jnp.concatenate([summed_in[c] for c in range(line)], axis=1)
+            product = sum_thirds(jnp.dot(thirds(mixed), acts(), preferred_element_type=F32))
+            own = first_image[here.y, here.x].reshape(rank, cols)
+            own = product * (1.0 / tokens) + RIDGE * own
+            mapped_image[here.y, here.x] = own.reshape(image_all.shape[3:])
+            mapped_x.start()
+
+        gram_x.received()
         first = 0
         for c in range(0, total_rank, LEAF):
             count = (total_rank - c) // tok // 8
-            panel = gram_ref[:, first : first + count].reshape(total_rank - c, LEAF)
+            panel = gram_at[:, first : first + count].reshape(total_rank - c, LEAF)
             m_ref[c:, c : c + LEAF] = panel * (1.0 / group_cols)
             first += count
 
-        proj_x.sent()
-        mixed_x.sent()
-        image_x.sent()
+        @pl.when(turn == 0)
+        def _():
+            mapped_x.middle()
 
         @pl.when(reducing)
         def _():
@@ -524,15 +626,17 @@
         def _():
             part_x.sent(reducers)
 
-        if tok > 1:
-            gram_x.sent()
+        gram_x.sent()
         factor_inverse(m_ref, w_ref)
 
-        @pl.when(turn < ITERS - 1)
-        def _():
-            at = pl.multiple_of(here.p * rank, rank)
-            image = image_ref[...].reshape(total_rank, cols)
-            basis_ref[...] = dot(w_ref[pl.ds(at, rank), :], image).astype(BF16)
+        @pl.when(turn == 0)
+        def _():
+            mapped_x.finish()
+            source = mapped_image[...].reshape(total_rank, cols)
+            upper = total_rank // 2
+            image[...] = jnp.concatenate(
+                [dot(w_ref[:upper, :upper], source[:upper]), dot(w_ref[upper:, :], source)], axis=0
+            ).reshape(image_all.shape[1:])
 
         return carry
 
@@ -546,7 +650,7 @@
     wide = turned.shape[0]
     per = wide // rows
     at = pl.multiple_of(here.p // per * wide, wide)
-    part = image_all[ITERS - 1, :, :, :, :, pl.ds(at, wide)].reshape(total_rank, wide)
+    part = image_all[1, :, :, :, :, pl.ds(at, wide)].reshape(total_rank, wide)
     turned[...] = dot(w_ref[...], part).T
     bases_ref[...] = turned[pl.ds(pl.multiple_of(here.p % per * rows, rows), rows), :]
     codes_x.received()
@@ -561,6 +665,8 @@
                 at = g * total_rank + h * half + c
                 latent_ref[:, at : at + size] = total[h * few : (h + 1) * few].astype(BF16)
     codes_x.sent()
+    for exchange in (proj_x, mixed_x, wide_x, summed_x, first_x, mapped_x):
+        exchange.sent()
 
 
 def turned_acts(full_ref, here):
@@ -603,8 +709,8 @@
         out_specs=(vmem(), vmem()),
         scratch_shapes=[
             pltpu.VMEM((side, side, 4, shard // 4, cols), BF16),
-            pltpu.VMEM((ITERS, side, side, 4, rank // 4, cols), F32),
-            pltpu.VMEM((tok, tiles, 8, LEAF), F32),
+            pltpu.VMEM((3, side, side, 4, rank // 4, cols), F32),
+            pltpu.VMEM((ITERS, tok, tiles, 8, LEAF), F32),
             pltpu.VMEM((rank, cols), BF16),
             pltpu.VMEM((rows, total_rank), F32),
             pltpu.VMEM(init_pieces, BF16),
@@ -617,6 +723,11 @@
             pltpu.VMEM((line, per_tile, 8, LEAF), F32),
             pltpu.VMEM((line, per_tile, 8, LEAF), F32),
             pltpu.VMEM((reducers, per_tile, 8, LEAF), F32),
+            pltpu.VMEM(pieces, F32),
+            pltpu.VMEM(pieces, F32),
+            pltpu.VMEM(pieces, F32),
+            pltpu.VMEM(pieces, F32),
+            pltpu.VMEM((3 * rank, cols), BF16),
             pltpu.VMEM((total_rank, total_rank), F32),
             pltpu.VMEM((total_rank, total_rank), F32),
             pltpu.VMEM((line * rank, line * rank), BF16),
@@ -625,11 +736,10 @@
             pltpu.VMEM((shard, total_rank), F32),
             pltpu.VMEM((max(rows, 128), total_rank), F32),
             pltpu.SemaphoreType.DMA((2,)),
-            pltpu.SemaphoreType.DMA((2, 7)),
+            pltpu.SemaphoreType.DMA((2, 10)),
             pltpu.SemaphoreType.DMA((2,)),
             pltpu.SemaphoreType.DMA((2, 20)),
-            pltpu.SemaphoreType.DMA((2,)),
-            pltpu.SemaphoreType.DMA((2, 20)),
+            pltpu.SemaphoreType.DMA((2, 2, 4)),
         ],
         compiler_params=params(0),
     )(acts.reshape(4, shard // 4, cols), init_basis[0], kept, member.reshape(1, -1))

time: 189 us -> 163 us (0.86)
  Pallas kernels: 186 us -> 160 us
    pallas_call x1, Pallas kernels: 186 us -> 160 us  [per_device(): pl.pallas_call(functools.partial(whole_kernel, groups, group_cols), out_s...]
where the time goes in v4:
time: 163 us
  Pallas kernels  160 us (98%)
  local copies, waits for them, and re-layouts  2.18 us (1%)
    pallas_call x1, Pallas kernels, per_device(): pl.pallas_call(functools.partial(whole_kernel, groups, group_cols), out_s...  160 us

profile of v4, /device:TPU:1, one launch (start us, length us, event | category | flops | bytes accessed | tf_op | source)
XLA Modules:
  0.0 163.0 jit_solution(6882332819386646447)
XLA Ops:
  0.6 160.2 %shard_map.59 = (f32[64,512]{1,0:T(8,128)}, bf16[8,1024]{1,0:T(8,128)(2,1)}) custom-call(bf16[4,32,1024]{2,1,0:T(8,128)(2,1)} %bitcast.4, f32[64,512]{1,0:T(8,128)} %bitcast.5, s32[16,16]{1,0:T(8,128)} %kept_ref.1, s32[1,16]{1,0:T(1,128)} %bitcast.7), custom_call_target="tpu_custom_call" | custom-call | tf_op jit(solution)/shard_map/pallas_call | solution.py:702
  160.8 0.0 copy-start
  160.8 1.6 copy.8
  162.4 0.0 copy-done
  162.4 0.6 copy.9
Async XLA Ops:
  160.8 1.6 copy-start

commit v5 on v4

--- a/solution.py
+++ b/solution.py
@@ -69,12 +69,16 @@
         pl.semaphore_wait(barrier, len(devices))
 
 
-def line_devices(here):
-    return [here.in_line((here.k + d) % here.line) for d in range(1, here.line)]
-
-
-def plane_devices(here):
-    return [here.in_plane((here.p + d) % here.tok) for d in range(1, here.tok)]
+def line_others(here):
+    steps = sorted(range(1, here.line), key=lambda d: -min(d, here.line - d))
+    return [lax.rem(here.k + d, here.line) for d in steps]
+
+
+def plane_others(here):
+    side = here.side
+    steps = [(dy, dx) for dy in range(side) for dx in range(side)][1:]
+    steps.sort(key=lambda d: -sum(min(a, side - a) for a in d))
+    return [lax.rem(here.y + dy, side) * side + lax.rem(here.x + dx, side) for dy, dx in steps]
 
 
 def ring_devices(here):
@@ -227,8 +231,9 @@
 
 
 class Exchange:
-    def __init__(self, at, count, device, src, dst, sems, which):
-        self.at, self.count, self.device = at, count, device
+    def __init__(self, at, others, device, src, dst, sems, which):
+        self.at, self.others, self.device = at, others, device
+        self.count = len(others) + 1
         self.src, self.dst, self.sems, self.which = src, dst, sems, which
 
     def send(self, to):
@@ -237,20 +242,15 @@
         ).start()
 
     def send_all(self):
-        def body(d, carry):
-            self.send(lax.rem(self.at + d, self.count))
-            return carry
-
-        lax.fori_loop(1, self.count, body, 0)
+        for other in self.others:
+            self.send(other)
 
     def keep(self):
         self.dst[self.at] = self.src[self.at]
 
     def all_of(self, ref, number):
-        other = lax.rem(self.at + 1, self.count)
-        return group_copy(
-            ref.at[pl.ds(0, number)], ref.at[pl.ds(0, number)], self.sems, self.which, self.device(other)
-        )
+        ref = ref.at[pl.ds(0, number)]
+        return group_copy(ref, ref, self.sems, self.which, self.device((self.others or [self.at])[0]))
 
     def received(self, number=None):
         number = self.count - 1 if number is None else number
@@ -282,9 +282,12 @@
         first = jnp.where(diag, jnp.where(lane - c0 == sub, 1.0, 0.0), here)
         full, low = first, first
         pivots = jnp.ones(shape, F32)
+        pivot = down(cols[0], 0)
         for j in range(HIGH):
-            pivot = down(cols[j], j)
             inverse = 1.0 / pivot
+            if j + 1 < HIGH:
+                cross = down(cols[j + 1], j) * down(cols[j], j + 1)
+                later = down(cols[j + 1], j + 1) - cross * inverse
             others = jnp.where(sub == j, 0.0, cols[j])
             below = jnp.where(sub > j, cols[j], 0.0)
             for k in range(j + 1, HIGH):
@@ -292,6 +295,8 @@
             full = full - (others * down(full, j)) * inverse
             low = low - (below * down(low, j)) * inverse
             pivots = jnp.where(sub == j, pivot, pivots)
+            if j + 1 < HIGH:
+                pivot = later
         solved = full / pivots
         done.append(jnp.where(lane < c0 + HIGH, low * lax.rsqrt(pivots), 0.0))
         if s + 1 < count:
@@ -316,7 +321,7 @@
     )
 
 
-def factor_inverse(m_ref, w_ref):
+def factor_inverse(m_ref, w_ref, others):
     size = m_ref.shape[0]
     w_ref[...] = jnp.zeros(w_ref.shape, F32)
 
@@ -328,6 +333,8 @@
 
             @pl.when(step == b)
             def _():
+                if b == 0:
+                    others()
                 inv = w_ref[r0:r1, r0:r1]
                 if r0:
                     left = dot(inv, m_ref[r0:r1, :r0])
@@ -413,6 +420,7 @@
     full_ref, image_all, gram_ref, basis_ref, init_v, init_out, init_in,
     proj_out, proj_in, mixed_out, mixed_in, part_out, part_in, sum_out, sum_in,
     wide_out, wide_in, summed_out, summed_in, thirds_ref,
+    own_ref, piece_out, piece_in, rows_out, rows_in,
     m_ref, w_ref, mix_ref, codes_out, codes_in, mapped, turned,
     local_sems, sems, xs, xr, cross_sems,
 ):
@@ -428,7 +436,8 @@
     init_copy = pltpu.make_async_copy(init_ref, init_v, local_sems.at[1])
     acts_copy.start()
     init_copy.start()
-    greet_start(line_devices(here) + plane_devices(here))
+    line_to, plane_to = line_others(here), plane_others(here)
+    greet_start([here.in_line(k) for k in line_to] + [here.in_plane(p) for p in plane_to])
     init_copy.wait()
     turned_init = init_v[...].T
     if tok > 1:
@@ -441,7 +450,7 @@
 
     acts_x = Gather(here, full_ref, xs, xr)
     acts_x.start()
-    spread = Exchange(here.p, tok, here.in_plane, init_out, init_in, sems, 0)
+    spread = Exchange(here.p, plane_to, here.in_plane, init_out, init_in, sems, 0)
     if tok > 1:
         spread.send_all()
         spread.keep()
@@ -465,7 +474,7 @@
     steps = line // per_step
 
     def line_exchange(src, dst, which):
-        return Exchange(here.k, line, here.in_line, src, dst, sems, which)
+        return Exchange(here.k, line_to, here.in_line, src, dst, sems, which)
 
     reducing = here.k < reducers
 
@@ -473,16 +482,16 @@
     mixed_x = line_exchange(mixed_out, mixed_in, 2)
     part_x = line_exchange(part_out, part_in, 3)
     sum_x = line_exchange(sum_out, sum_in, 4)
-    codes_x = line_exchange(codes_out, codes_in, 7)
-    wide_x = line_exchange(wide_out, wide_in, 8)
-    summed_x = line_exchange(summed_out, summed_in, 9)
-    first_image, image, mapped_image = (image_all.at[n] for n in range(3))
-    first_x = Cross(here, first_image, cross_sems.at[0])
-    mapped_x = Cross(here, mapped_image, cross_sems.at[1])
+    codes_x = line_exchange(codes_out, codes_in, 9)
+    wide_x = line_exchange(wide_out, wide_in, 10)
+    summed_x = line_exchange(summed_out, summed_in, 11)
+    image_ref, mapped_image = image_all.at[0], image_all.at[1]
+    mapped_x = Cross(here, mapped_image, cross_sems)
 
     def project(basis, finish, exchange):
         def body(d, carry):
-            u = (here.k // per_step + 1 + d) % steps
+            away = steps // 2 + (2 * (d % 2) - 1) * ((d + 1) // 2)
+            u = (here.k // per_step + away) % steps
             proj = finish(
                 lax.dot_general(
                     basis[...], tokens_at(full_ref, u, per_step * chunk),
@@ -519,36 +528,67 @@
     mixed = jnp.concatenate([mixed_in[c] for c in range(line)], axis=1)
     own = jnp.dot(mixed, acts(), preferred_element_type=F32)
     own = own * (1.0 / tokens) + RIDGE * basis_ref[...].astype(F32)
-    first_image[here.y, here.x] = own.reshape(image_all.shape[3:])
-    first_x.start()
+    own_ref[...] = own
+    chunks, split = piece_out.shape[0], tok // piece_out.shape[0]
+    width = cols // chunks
+    for c in range(chunks):
+        piece_out[c] = own[:, c * width : (c + 1) * width]
+    for to in plane_to:
+        group_copy(
+            piece_out.at[to // split], piece_in.at[here.p], sems, 12, here.in_plane(to)
+        ).start()
+    piece_in[here.p] = piece_out[here.p // split]
     thirds_ref[...] = thirds(own)
     project(thirds_ref, sum_thirds, wide_x)
-    first_x.middle()
-    first_x.finish()
+
+    if tok > 1:
+        arrived = piece_in.at[pl.ds(0, tok - 1)]
+        piece_copy = group_copy(arrived, arrived, sems, 12, here.in_plane(plane_to[0]))
+        piece_copy.wait_recv()
+    kind, slot = here.p % split, here.p // split
+    tile_at = 0
+    for c in range(0, total_rank, LEAF):
+        high = (total_rank - c) // tok
+        mine = []
+        for m in range(chunks):
+            for r in range(0, high, 8):
+                row = c + (split * m + kind) * high + r
+                mine.append(piece_in[row // rank, pl.ds(pl.multiple_of(row % rank, 8), 8)])
+        panel = piece_in[c // rank : (c + LEAF) // rank].reshape(LEAF, width)
+        tile = dot_t(jnp.concatenate(mine, axis=0), panel)
+        rows_out[:, tile_at : tile_at + high // 8] = tile.reshape(chunks, high // 8, 8, LEAF)
+        tile_at += high // 8
+    for d in sorted(range(1, chunks), key=lambda d: -min(d, chunks - d)):
+        to = lax.rem(slot + d, chunks)
+        group_copy(
+            rows_out.at[to], rows_in.at[slot], sems, 13, here.in_plane(split * to + kind)
+        ).start()
+    rows_in[slot] = rows_out[slot]
+    if tok > 1:
+        arrived = rows_in.at[pl.ds(0, chunks - 1)]
+        rows_copy = group_copy(arrived, arrived, sems, 13, here.in_plane(plane_to[0]))
+        rows_copy.wait_recv()
+    part_out[...] = jnp.sum(rows_in[...], axis=0).reshape(part_out.shape)
 
     def iteration(turn, carry):
-        image_ref = image_all.at[turn]
         gram_at = gram_ref.at[turn]
 
-        whole = image_ref[...].reshape(total_rank, cols)
-        tiles = []
-        for c in range(0, total_rank, LEAF):
-            high = (total_rank - c) // tok
-            mine = [eight_rows(image_ref, c + here.p * high + r) for r in range(0, high, 8)]
-            tile = dot_t(jnp.concatenate(mine, axis=0), whole[c : c + LEAF])
-            tiles.append(tile.reshape(high // 8, 8, LEAF))
-        part_out[...] = jnp.concatenate(tiles, axis=0).reshape(part_out.shape)
-
-        def send_part(d, carry):
-            to = lax.rem(here.k + d, line)
+        @pl.when(turn > 0)
+        def _():
+            whole = image_ref[...].reshape(total_rank, cols)
+            tiles = []
+            for c in range(0, total_rank, LEAF):
+                high = (total_rank - c) // tok
+                mine = [eight_rows(image_ref, c + here.p * high + r) for r in range(0, high, 8)]
+                tile = dot_t(jnp.concatenate(mine, axis=0), whole[c : c + LEAF])
+                tiles.append(tile.reshape(high // 8, 8, LEAF))
+            part_out[...] = jnp.concatenate(tiles, axis=0).reshape(part_out.shape)
+
+        for to in line_to:
 
             @pl.when(to < reducers)
             def _():
                 part_x.send(to)
-
-            return carry
-
-        lax.fori_loop(1, line, send_part, 0)
 
         @pl.when(turn == 0)
         def _():
@@ -585,33 +625,41 @@
             sum_x.received(reducers)
 
         gram_at[here.p] = sum_in[...].reshape(gram_ref.shape[2:])
-        gram_x = Exchange(here.p, tok, here.in_plane, gram_at, gram_at, sems, 5 + turn)
+        front = total_rank // tok // 8
+        spans = [(0, front), (front, gram_ref.shape[2] - front)]
+
+        def gram_copy(n, ref, to):
+            return group_copy(ref, ref, sems, 5 + 2 * turn + n, here.in_plane(to))
+
+        def gram_whole(n):
+            return gram_copy(n, gram_at.at[pl.ds(0, tok - 1), pl.ds(*spans[n])], plane_to[0])
+
         if tok > 1:
-            def send_gram(d, carry):
-                to = lax.rem(here.p + d, tok)
-                mine = gram_at.at[here.p]
-                group_copy(mine, mine, sems, 5 + turn, here.in_plane(to)).start()
-                return carry
-
-            lax.fori_loop(1, tok, send_gram, 0)
+            for n in (0, 1):
+                for to in plane_to:
+                    gram_copy(n, gram_at.at[here.p, pl.ds(*spans[n])], to).start()
 
         @pl.when(turn == 0)
         def _():
             summed_x.received()
             mixed = jnp.concatenate([summed_in[c] for c in range(line)], axis=1)
             product = sum_thirds(jnp.dot(thirds(mixed), acts(), preferred_element_type=F32))
-            own = first_image[here.y, here.x].reshape(rank, cols)
-            own = product * (1.0 / tokens) + RIDGE * own
+            own = product * (1.0 / tokens) + RIDGE * own_ref[...]
             mapped_image[here.y, here.x] = own.reshape(image_all.shape[3:])
             mapped_x.start()
 
-        gram_x.received()
-        first = 0
-        for c in range(0, total_rank, LEAF):
-            count = (total_rank - c) // tok // 8
-            panel = gram_at[:, first : first + count].reshape(total_rank - c, LEAF)
-            m_ref[c:, c : c + LEAF] = panel * (1.0 / group_cols)
-            first += count
+        def panels(n):
+            if tok > 1:
+                gram_whole(n).wait_recv()
+            first = 0
+            for c in range(0, total_rank, LEAF):
+                count = (total_rank - c) // tok // 8
+                if (c > 0) == (n > 0):
+                    panel = gram_at[:, first : first + count].reshape(total_rank - c, LEAF)
+                    m_ref[c:, c : c + LEAF] = panel * (1.0 / group_cols)
+                first += count
+
+        panels(0)
 
         @pl.when(turn == 0)
         def _():
@@ -626,15 +674,17 @@
         def _():
             part_x.sent(reducers)
 
-        gram_x.sent()
-        factor_inverse(m_ref, w_ref)
+        factor_inverse(m_ref, w_ref, lambda: panels(1))
+        if tok > 1:
+            for n in (0, 1):
+                gram_whole(n).wait_send()
 
         @pl.when(turn == 0)
         def _():
             mapped_x.finish()
             source = mapped_image[...].reshape(total_rank, cols)
             upper = total_rank // 2
-            image[...] = jnp.concatenate(
+            image_ref[...] = jnp.concatenate(
                 [dot(w_ref[:upper, :upper], source[:upper]), dot(w_ref[upper:, :], source)], axis=0
             ).reshape(image_all.shape[1:])
 
@@ -650,7 +700,7 @@
     wide = turned.shape[0]
     per = wide // rows
     at = pl.multiple_of(here.p // per * wide, wide)
-    part = image_all[1, :, :, :, :, pl.ds(at, wide)].reshape(total_rank, wide)
+    part = image_all[0, :, :, :, :, pl.ds(at, wide)].reshape(total_rank, wide)
     turned[...] = dot(w_ref[...], part).T
     bases_ref[...] = turned[pl.ds(pl.multiple_of(here.p % per * rows, rows), rows), :]
     codes_x.received()
@@ -665,8 +715,11 @@
                 at = g * total_rank + h * half + c
                 latent_ref[:, at : at + size] = total[h * few : (h + 1) * few].astype(BF16)
     codes_x.sent()
-    for exchange in (proj_x, mixed_x, wide_x, summed_x, first_x, mapped_x):
+    for exchange in (proj_x, mixed_x, wide_x, summed_x, mapped_x):
         exchange.sent()
+    if tok > 1:
+        piece_copy.wait_send()
+        rows_copy.wait_send()
 
 
 def turned_acts(full_ref, here):
@@ -696,6 +749,7 @@
     tiles = sum((total_rank - c) // tok // 8 for c in range(0, total_rank, LEAF))
     reducers = max(d for d in range(1, line + 1) if tiles % d == 0)
     per_tile = tiles // reducers
+    chunks = max(1, tok // 2)
     pieces = (line, rank, tokens // line)
     init_pieces = (tok, rank, 128)
     codes = (line, shard // line * 2, total_rank // 2)
@@ -709,7 +763,7 @@
         out_specs=(vmem(), vmem()),
         scratch_shapes=[
             pltpu.VMEM((side, side, 4, shard // 4, cols), BF16),
-            pltpu.VMEM((3, side, side, 4, rank // 4, cols), F32),
+            pltpu.VMEM((2, side, side, 4, rank // 4, cols), F32),
             pltpu.VMEM((ITERS, tok, tiles, 8, LEAF), F32),
             pltpu.VMEM((rank, cols), BF16),
             pltpu.VMEM((rows, total_rank), F32),
@@ -728,6 +782,11 @@
             pltpu.VMEM(pieces, F32),
             pltpu.VMEM(pieces, F32),
             pltpu.VMEM((3 * rank, cols), BF16),
+            pltpu.VMEM((rank, cols), F32),
+            pltpu.VMEM((chunks, rank, cols // chunks), F32),
+            pltpu.VMEM((tok, rank, cols // chunks), F32),
+            pltpu.VMEM((chunks, tiles, 8, LEAF), F32),
+            pltpu.VMEM((chunks, tiles, 8, LEAF), F32),
             pltpu.VMEM((total_rank, total_rank), F32),
             pltpu.VMEM((total_rank, total_rank), F32),
             pltpu.VMEM((line * rank, line * rank), BF16),
@@ -736,10 +795,10 @@
             pltpu.VMEM((shard, total_rank), F32),
             pltpu.VMEM((max(rows, 128), total_rank), F32),
             pltpu.SemaphoreType.DMA((2,)),
-            pltpu.SemaphoreType.DMA((2, 10)),
+            pltpu.SemaphoreType.DMA((2, 14)),
             pltpu.SemaphoreType.DMA((2,)),
             pltpu.SemaphoreType.DMA((2, 20)),
-            pltpu.SemaphoreType.DMA((2, 2, 4)),
+            pltpu.SemaphoreType.DMA((2, 4)),
         ],
         compiler_params=params(0),
     )(acts.reshape(4, shard // 4, cols), init_basis[0], kept, member.reshape(1, -1))

time: 163 us -> 150 us (0.920)
  Pallas kernels: 160 us -> 147 us
    pallas_call x1, Pallas kernels: 160 us -> 147 us  [per_device(): pl.pallas_call(functools.partial(whole_kernel, groups, group_cols), out_s...]
where the time goes in v5:
time: 150 us
  Pallas kernels  147 us (98%)
  local copies, waits for them, and re-layouts  2.18 us (1%)
    pallas_call x1, Pallas kernels, per_device(): pl.pallas_call(functools.partial(whole_kernel, groups, group_cols), out_s...  147 us

profile of v5, /device:TPU:1, one launch (start us, length us, event | category | flops | bytes accessed | tf_op | source)
XLA Modules:
  0.0 149.6 jit_solution(7621937144620595532)
XLA Ops:
  0.6 146.7 %shard_map.59 = (f32[64,512]{1,0:T(8,128)}, bf16[8,1024]{1,0:T(8,128)(2,1)}) custom-call(bf16[4,32,1024]{2,1,0:T(8,128)(2,1)} %bitcast.4, f32[64,512]{1,0:T(8,128)} %bitcast.5, s32[16,16]{1,0:T(8,128)} %kept_ref.1, s32[1,16]{1,0:T(1,128)} %bitcast.7), custom_call_target="tpu_custom_call" | custom-call | tf_op jit(solution)/shard_map/pallas_call | solution.py:756
  147.4 0.0 copy-start
  147.4 1.6 %copy.8 = f32[1,64,512]{2,1,0:T(8,128)} copy(f32[1,64,512]{2,1,0:T(8,128)} %bitcast.6) | data formatting | bytes 262144
  149.0 0.0 copy-done
  149.0 0.6 copy.9
Async XLA Ops:
  147.4 1.6 %copy-start = (bf16[8,1024]{1,0:T(8,128)(2,1)S(1)}, bf16[8,1024]{1,0:T(8,128)(2,1)}, u32[]{:S(2)}) copy-start(bf16[8,1024]{1,0:T(8,128)(2,1)} %get-tuple-element.9) | copy-start | bytes 49156

commit v6 on v5

--- a/solution.py
+++ b/solution.py
@@ -315,6 +315,20 @@
     return jnp.dot(a, b, precision=HIGHEST, preferred_element_type=F32)
 
 
+def halves(x):
+    high = x.astype(BF16)
+    return high, (x - high.astype(F32)).astype(BF16)
+
+
+def dot3(a, b):
+    (ah, al), (bh, bl) = halves(a), halves(b)
+
+    def product(p, q):
+        return jnp.dot(p, q, preferred_element_type=F32)
+
+    return product(ah, bh) + (product(ah, bl) + product(al, bh))
+
+
 def dot_t(a, b):
     return lax.dot_general(
         a, b, (((1,), (1,)), ((), ())), precision=HIGHEST, preferred_element_type=F32
@@ -333,8 +347,8 @@
 
             @pl.when(step == b)
             def _():
-                if b == 0:
-                    others()
+                if b < 2:
+                    others(b)
                 inv = w_ref[r0:r1, r0:r1]
                 if r0:
                     left = dot(inv, m_ref[r0:r1, :r0])
@@ -415,9 +429,9 @@
 
 def whole_kernel(
     groups, group_cols,
-    acts_ref, init_ref, kept_ref, member_ref,
+    acts_ref, init_ref, kept_hbm, member_hbm,
     bases_ref, latent_ref,
-    full_ref, image_all, gram_ref, basis_ref, init_v, init_out, init_in,
+    kept_ref, member_ref, full_ref, image_all, gram_ref, basis_ref, init_v, init_out, init_in,
     proj_out, proj_in, mixed_out, mixed_in, part_out, part_in, sum_out, sum_in,
     wide_out, wide_in, summed_out, summed_in, thirds_ref,
     own_ref, piece_out, piece_in, rows_out, rows_in,
@@ -434,8 +448,10 @@
 
     acts_copy = pltpu.make_async_copy(acts_ref, turned_acts(full_ref, here), local_sems.at[0])
     init_copy = pltpu.make_async_copy(init_ref, init_v, local_sems.at[1])
-    acts_copy.start()
-    init_copy.start()
+    kept_copy = pltpu.make_async_copy(kept_hbm, kept_ref, local_sems.at[2])
+    member_copy = pltpu.make_async_copy(member_hbm, member_ref, local_sems.at[3])
+    for copy in (acts_copy, init_copy, kept_copy, member_copy):
+        copy.start()
     line_to, plane_to = line_others(here), plane_others(here)
     greet_start([here.in_line(k) for k in line_to] + [here.in_plane(p) for p in plane_to])
     init_copy.wait()
@@ -454,6 +470,8 @@
     if tok > 1:
         spread.send_all()
         spread.keep()
+    kept_copy.wait()
+    member_copy.wait()
     same, member_masks = masks(member_ref, line, groups)
     linked = jnp.where(same, kept_ref[...].astype(F32), 0.0)
     mix_ref[...] = mixing(linked, rank)
@@ -661,9 +679,14 @@
 
         panels(0)
 
-        @pl.when(turn == 0)
-        def _():
-            mapped_x.middle()
+        def more(b):
+            if b == 0:
+                panels(1)
+                return
+
+            @pl.when(turn == 0)
+            def _():
+                mapped_x.middle()
 
         @pl.when(reducing)
         def _():
@@ -674,7 +697,7 @@
         def _():
             part_x.sent(reducers)
 
-        factor_inverse(m_ref, w_ref, lambda: panels(1))
+        factor_inverse(m_ref, w_ref, more)
         if tok > 1:
             for n in (0, 1):
                 gram_whole(n).wait_send()
@@ -685,7 +708,7 @@
             source = mapped_image[...].reshape(total_rank, cols)
             upper = total_rank // 2
             image_ref[...] = jnp.concatenate(
-                [dot(w_ref[:upper, :upper], source[:upper]), dot(w_ref[upper:, :], source)], axis=0
+                [dot3(w_ref[:upper, :upper], source[:upper]), dot3(w_ref[upper:, :], source)], axis=0
             ).reshape(image_all.shape[1:])
 
         return carry
@@ -759,9 +782,11 @@
             jax.ShapeDtypeStruct((rows, total_rank), F32),
             jax.ShapeDtypeStruct((shard // line, groups * total_rank), BF16),
         ),
-        in_specs=[pl.BlockSpec(memory_space=pl.ANY), pl.BlockSpec(memory_space=pl.ANY), vmem(), vmem()],
+        in_specs=[pl.BlockSpec(memory_space=pl.ANY)] * 4,
         out_specs=(vmem(), vmem()),
         scratch_shapes=[
+            pltpu.VMEM(kept.shape, kept.dtype),
+            pltpu.VMEM((1, kept.shape[0]), member.dtype),
             pltpu.VMEM((side, side, 4, shard // 4, cols), BF16),
             pltpu.VMEM((2, side, side, 4, rank // 4, cols), F32),
             pltpu.VMEM((ITERS, tok, tiles, 8, LEAF), F32),
@@ -794,7 +819,7 @@
             pltpu.VMEM(codes, BF16),
             pltpu.VMEM((shard, total_rank), F32),
             pltpu.VMEM((max(rows, 128), total_rank), F32),
-            pltpu.SemaphoreType.DMA((2,)),
+            pltpu.SemaphoreType.DMA((4,)),
             pltpu.SemaphoreType.DMA((2, 14)),
             pltpu.SemaphoreType.DMA((2,)),
             pltpu.SemaphoreType.DMA((2, 20)),

time: 150 us -> 143 us (0.953)
  Pallas kernels: 147 us -> 139 us
    pallas_call x1, Pallas kernels: 147 us -> 139 us  [per_device(): pl.pallas_call(functools.partial(whole_kernel, groups, group_cols), out_s...]
where the time goes in v6:
time: 143 us; the launch traced here: 142 us
  Pallas kernels  139 us (97%)
  local copies, waits for them, and re-layouts  2.18 us (2%)
    pallas_call x1, Pallas kernels, per_device(): pl.pallas_call(functools.partial(whole_kernel, groups, group_cols), out_s...  139 us

profile of v6, /device:TPU:1, one launch (start us, length us, event | category | flops | bytes accessed | tf_op | source)
XLA Modules:
  0.0 142.3 jit_solution(16380886729899207998)
XLA Ops:
  0.6 139.4 %shard_map.59 = (f32[64,512]{1,0:T(8,128)}, bf16[8,1024]{1,0:T(8,128)(2,1)}) custom-call(bf16[4,32,1024]{2,1,0:T(8,128)(2,1)} %bitcast.4, f32[64,512]{1,0:T(8,128)} %bitcast.5, s32[16,16]{1,0:T(8,128)} %kept_hbm.1, s32[1,16]{1,0:T(1,128)} %bitcast.7), custom_call_target="tpu_custom_call" | custom-call | tf_op jit(solution)/shard_map/pallas_call | solution.py:779
  140.1 0.0 copy-start
  140.1 1.6 %copy.8 = f32[1,64,512]{2,1,0:T(8,128)} copy(f32[1,64,512]{2,1,0:T(8,128)} %bitcast.6) | data formatting | bytes 262144
  141.7 0.0 copy-done
  141.7 0.6 copy.9
Async XLA Ops:
  140.1 1.6 %copy-start = (bf16[8,1024]{1,0:T(8,128)(2,1)S(1)}, bf16[8,1024]{1,0:T(8,128)(2,1)}, u32[]{:S(2)}) copy-start(bf16[8,1024]{1,0:T(8,128)(2,1)} %get-tuple-element.9) | copy-start | bytes 49156

commit v7 on v6

--- a/solution.py
+++ b/solution.py
@@ -351,7 +351,7 @@
                     others(b)
                 inv = w_ref[r0:r1, r0:r1]
                 if r0:
-                    left = dot(inv, m_ref[r0:r1, :r0])
+                    left = dot3(inv, m_ref[r0:r1, :r0])
                     w_ref[r0:r1, :r0] = left
                 if r1 < size:
                     back = dot_t(m_ref[r1:, r0:r1], inv)
@@ -359,9 +359,9 @@
                         m_ref[c:, c : c + LEAF] -= dot_t(
                             back[c - r1 :], back[c - r1 : c - r1 + LEAF]
                         )
-                    m_ref[r1:, r0:r1] = -dot(back, inv)
+                    m_ref[r1:, r0:r1] = -dot3(back, inv)
                     if r0:
-                        m_ref[r1:, :r0] -= dot(back, left)
+                        m_ref[r1:, :r0] -= dot3(back, left)
 
         return carry
 
@@ -478,14 +478,12 @@
     acts_x.finish()
     if tok > 1:
         spread.received()
-        spread.sent()
         per = 128 // rows
         for c in range(tok // per):
             total = init_in[c * per].astype(F32)
             for d in range(1, per):
                 total += pltpu.roll(init_in[c * per + d].astype(F32), d * rows, 1)
             basis_ref[:, c * 128 : c * 128 + 128] = total.astype(BF16)
-    acts_x.sent()
 
     chunk = tokens // line
     per_step = 2 if line % 2 == 0 else 1
@@ -726,6 +724,12 @@
     part = image_all[0, :, :, :, :, pl.ds(at, wide)].reshape(total_rank, wide)
     turned[...] = dot(w_ref[...], part).T
     bases_ref[...] = turned[pl.ds(pl.multiple_of(here.p % per * rows, rows), rows), :]
+    for exchange in (acts_x, proj_x, mixed_x, wide_x, summed_x, mapped_x):
+        exchange.sent()
+    if tok > 1:
+        spread.sent()
+        piece_copy.wait_send()
+        rows_copy.wait_send()
     codes_x.received()
     scale = 1.0 / math.sqrt(group_cols)
     few = latent_ref.shape[0]
@@ -738,11 +742,6 @@
                 at = g * total_rank + h * half + c
                 latent_ref[:, at : at + size] = total[h * few : (h + 1) * few].astype(BF16)
     codes_x.sent()
-    for exchange in (proj_x, mixed_x, wide_x, summed_x, mapped_x):
-        exchange.sent()
-    if tok > 1:
-        piece_copy.wait_send()
-        rows_copy.wait_send()
 
 
 def turned_acts(full_ref, here):

time: 143 us -> 142 us (level)
  no operation moved by 1% of the time
where the time goes in v7:
time: 142 us
  Pallas kernels  139 us (98%)
  local copies, waits for them, and re-layouts  2.18 us (2%)
    pallas_call x1, Pallas kernels, per_device(): pl.pallas_call(functools.partial(whole_kernel, groups, group_cols), out_s...  139 us

profile of v7, /device:TPU:1, one launch (start us, length us, event | category | flops | bytes accessed | tf_op | source)
XLA Modules:
  0.0 142.3 jit_solution(4935436153873847910)
XLA Ops:
  0.6 139.4 %shard_map.59 = (f32[64,512]{1,0:T(8,128)}, bf16[8,1024]{1,0:T(8,128)(2,1)}) custom-call(bf16[4,32,1024]{2,1,0:T(8,128)(2,1)} %bitcast.4, f32[64,512]{1,0:T(8,128)} %bitcast.5, s32[16,16]{1,0:T(8,128)} %kept_hbm.1, s32[1,16]{1,0:T(1,128)} %bitcast.7), custom_call_target="tpu_custom_call" | custom-call | tf_op jit(solution)/shard_map/pallas_call | solution.py:778
  140.1 0.0 copy-start
  140.1 1.6 %copy.8 = f32[1,64,512]{2,1,0:T(8,128)} copy(f32[1,64,512]{2,1,0:T(8,128)} %bitcast.6) | data formatting | bytes 262144
  141.6 0.0 copy-done
  141.6 0.6 copy.9
Async XLA Ops:
  140.1 1.6 %copy-start = (bf16[8,1024]{1,0:T(8,128)(2,1)S(1)}, bf16[8,1024]{1,0:T(8,128)(2,1)}, u32[]{:S(2)}) copy-start(bf16[8,1024]{1,0:T(8,128)(2,1)} %get-tuple-element.9) | copy-start | bytes 49156
